TPU v7x, 32 devices: a whole 2x2x4 slice. The times are simulated.
32 devices in a mesh: grp: 2 (over x), head: 2 (over y), blk: 8 (over z, core).
Axes of the slice: x: 2, y: 2, z: 4, core: 2. Of those that a mesh axis runs over, the one named last changes fastest.
Arguments:
- tokens_in: bfloat16 [4096, 768], P(('grp', 'head', 'blk')), may hold values from -6 to 6
- norm_gains: bfloat16 [2, 768], P(None, ('grp', 'head')), may hold values from 0.5 to 1.5
- attn_qkv: bfloat16 [768, 2304], P(None, ('grp', 'head')), may hold values from -0.21875 to 0.21875
- attn_proj: bfloat16 [768, 768], P(None, ('grp', 'head')), may hold values from -0.875 to 0.875
- router_rows: bfloat16 [16, 768], P(None, ('grp', 'head')), may hold values from -0.15917969 to 0.15917969
- shared_gate_up: bfloat16 [768, 4096], P(None, ('grp', 'head')), may hold values from -0.21875 to 0.21875
- shared_down: bfloat16 [2048, 768], P(None, ('grp', 'head')), may hold values from -0.1875 to 0.1875
- expert_gate_up: bfloat16 [2, 768, 32768], P(None, ('grp', 'head'), 'blk'), may hold values from -0.21875 to 0.21875
- expert_down: bfloat16 [32768, 768], P('blk', ('grp', 'head')), may hold values from -1 to 1
- routes: int32 [4096, 2], P(('grp', 'head', 'blk')), may hold values from 0 to 15, all different within a row; in each aligned block of 128 rows (0 to 127, 128 to 255, ...) at most 20 rows name the same one
- out_grad: bfloat16 [4096, 768], P(('grp', 'head', 'blk')), may hold values from -6 to 6
Outputs:
- layer_out: bfloat16 [4096, 768], P(('grp', 'head', 'blk'))
- grad_tokens: float32 [4096, 768], P(('grp', 'head', 'blk'))
- grad_gains: float32 [2, 768], P(None, ('grp', 'head'))
- grad_qkv: float32 [768, 2304], P(None, ('grp', 'head'))
- grad_proj: float32 [768, 768], P(None, ('grp', 'head'))
- grad_router: float32 [16, 768], P(None, ('grp', 'head'))
- grad_shared_gate_up: float32 [768, 4096], P(None, ('grp', 'head'))
- grad_shared_down: float32 [2048, 768], P(None, ('grp', 'head'))
- grad_expert_gate_up: float32 [2, 768, 32768], P(None, ('grp', 'head'), 'blk')
- grad_expert_down: float32 [32768, 768], P('blk', ('grp', 'head'))
Inputs may be any that keep to these rules, and one draw needn't show every extreme that they name: `routes`: each row names two different experts; among the rows of one device (aligned blocks of 128 rows) no expert is named more than 20 times, a bound that some block reaches.
All inputs are finite; a program needn't handle non-finite values.
Results may differ from a plain program's by a relative error of at most 0.018.
Values may be sent and summed in bfloat16 or wider, within the bound.
No kernel may reach another device: no remote copies, remote signals or barrier semaphores. Data moves between devices by JAX's collectives and lax.ppermute only.
A program may use at most 192 MiB of HBM per device.

v0:
```python
import jax
import jax.numpy as jnp
from jax import lax
from jax.sharding import PartitionSpec as P

HEADS = 12
DH = 64
EXPERTS = 16
FF = 2048
SFF = 2048
PROMPT_ROWS = 64
PROMPT_LEAST = 1024


EPSILON = 1e-06
NEGATIVE = -1e30


def norm_rows(values, gain):
    inverse = lax.rsqrt(jnp.mean(values * values, axis=-1, keepdims=True) + EPSILON)
    return (values * inverse * gain, inverse)


def norm_back(values, inverse, gain, upstream):
    scaled = upstream * gain
    inner_mean = jnp.mean(scaled * values, axis=-1, keepdims=True)
    return (
        inverse * scaled - values * inverse**3 * inner_mean,
        jnp.sum(upstream * values * inverse, axis=0),
    )


def angle_tables(positions):
    step_index = jnp.arange(DH // 2, dtype=jnp.float32)
    freq_rates = 10000.0 ** (-2.0 * step_index / DH)
    angles = positions.astype(jnp.float32)[:, None] * freq_rates[None, :]
    return (jnp.cos(angles)[:, None, :], jnp.sin(angles)[:, None, :])


def rotate(values, cosine, sine_table):
    half_size = values.shape[-1] // 2
    first_half = values[..., :half_size]
    second = values[..., half_size:]
    return jnp.concatenate(
        [first_half * cosine - second * sine_table, second * cosine + first_half * sine_table],
        axis=-1,
    )


def swish_parts(gate_value):
    sigmoid = jax.nn.sigmoid(gate_value)
    return (gate_value * sigmoid, sigmoid * (1.0 + gate_value * (1.0 - sigmoid)))


def row_layout(head_part, within, block_index, heads_axis, blocks_axis, row_count, prompt_dev):
    prompt_all = prompt_dev * heads_axis * blocks_axis
    is_prompt = within < prompt_dev
    prompt_index = (block_index * heads_axis + head_part) * prompt_dev + within
    cont_index = head_part * (row_count - prompt_dev) + within - prompt_dev
    positions = jnp.where(is_prompt, prompt_index, prompt_all + cont_index)
    return (is_prompt, prompt_index, cont_index, positions)


def fetch_weights(
    norm_gains,
    attn_qkv,
    attn_proj,
    router_rows,
    shared_gate_up,
    shared_down,
    expert_gate_up,
    expert_down,
):
    return (
        lax.all_gather(norm_gains, ("grp", "head"), axis=1, tiled=True),
        lax.all_gather(attn_qkv, ("grp", "head"), axis=1, tiled=True),
        lax.all_gather(attn_proj, ("grp", "head"), axis=1, tiled=True),
        lax.all_gather(router_rows, ("grp", "head"), axis=1, tiled=True),
        lax.all_gather(shared_gate_up, ("grp", "head"), axis=1, tiled=True),
        lax.all_gather(shared_down, ("grp", "head"), axis=1, tiled=True),
        lax.all_gather(expert_gate_up, ("grp", "head"), axis=1, tiled=True),
        lax.all_gather(expert_down, ("grp", "head"), axis=1, tiled=True),
    )


def masked_scores(queries, key_rows, visible):
    scores = jnp.einsum(
        "qhd,khd->hqk", queries, key_rows, preferred_element_type=jnp.float32
    ) * DH ** (-0.5)
    return jnp.where(visible[None], scores, NEGATIVE)


def add_stats(carry, scores, visible):
    row_peak, row_total = carry
    new_peak = jnp.maximum(row_peak, jnp.max(scores, axis=-1))
    terms = jnp.where(visible[None], jnp.exp(scores - new_peak[:, :, None]), 0.0)
    return (new_peak, row_total * jnp.exp(row_peak - new_peak) + jnp.sum(terms, axis=-1))


def block_probs(scores, visible, log_total):
    return jnp.where(visible[None], jnp.exp(scores - log_total[:, :, None]), 0.0)


def grad_block(queries, grad_out, log_total, delta, key_rows, value_rows, visible):
    scale_factor = DH ** (-0.5)
    soft_weights = block_probs(masked_scores(queries, key_rows, visible), visible, log_total)
    grad_weights = jnp.einsum(
        "qhd,khd->hqk", grad_out, value_rows, preferred_element_type=jnp.float32
    )
    grad_scores = (soft_weights * (grad_weights - delta[:, :, None])).astype(jnp.bfloat16)
    grad_query = (
        jnp.einsum("hqk,khd->qhd", grad_scores, key_rows, preferred_element_type=jnp.float32)
        * scale_factor
    )
    grad_key = (
        jnp.einsum("hqk,qhd->khd", grad_scores, queries, preferred_element_type=jnp.float32)
        * scale_factor
    )
    grad_value = jnp.einsum(
        "hqk,qhd->khd",
        soft_weights.astype(jnp.bfloat16),
        grad_out,
        preferred_element_type=jnp.float32,
    )
    return (grad_query, grad_key, grad_value)


def body(
    tokens_in,
    norm_gains,
    attn_qkv,
    attn_proj,
    router_rows,
    shared_gate_up,
    shared_down,
    expert_gate_up,
    expert_down,
    routes,
    out_grad,
):
    heads_axis = lax.axis_size("head")
    blocks_axis = lax.axis_size("blk")
    row_count = tokens_in.shape[0]
    width_all = tokens_in.shape[1]
    prompt_dev = max(PROMPT_ROWS, PROMPT_LEAST // (heads_axis * blocks_axis))
    prompt_all = prompt_dev * heads_axis * blocks_axis
    local_heads = HEADS // heads_axis
    query_rows = heads_axis * row_count
    key_block = min(512, prompt_all)
    block_count = prompt_all // key_block
    head_me = lax.axis_index("head")
    block_me = lax.axis_index("blk")
    gain_rows, qkv_w, proj_w, router_w, shared_w, shared_out_w, expert_w, expert_out_w = (
        fetch_weights(
            norm_gains,
            attn_qkv,
            attn_proj,
            router_rows,
            shared_gate_up,
            shared_down,
            expert_gate_up,
            expert_down,
        )
    )
    tokens = tokens_in.astype(jnp.float32)
    first_gain = gain_rows[0].astype(jnp.float32)
    second_gain = gain_rows[1].astype(jnp.float32)
    normed_f, first_inverse = norm_rows(tokens, first_gain)
    normed = normed_f.astype(jnp.bfloat16)
    mixed_qkv = jnp.dot(normed, qkv_w, preferred_element_type=jnp.float32)
    token_row = jnp.arange(row_count, dtype=jnp.int32)
    token_pos = row_layout(
        head_me, token_row, block_me, heads_axis, blocks_axis, row_count, prompt_dev
    )[3]
    token_cos, token_sin = angle_tables(token_pos)
    query_tok = (
        rotate(mixed_qkv[:, :width_all].reshape(row_count, HEADS, DH), token_cos, token_sin)
        .reshape(row_count, width_all)
        .astype(jnp.bfloat16)
    )
    key_tok = (
        rotate(
            mixed_qkv[:, width_all : 2 * width_all].reshape(row_count, HEADS, DH),
            token_cos,
            token_sin,
        )
        .reshape(row_count, width_all)
        .astype(jnp.bfloat16)
    )
    value_tok = mixed_qkv[:, 2 * width_all :].astype(jnp.bfloat16)
    query_head, key_head, value_head = (
        lax.all_to_all(query_tok, "head", split_axis=1, concat_axis=0, tiled=True),
        lax.all_to_all(key_tok, "head", split_axis=1, concat_axis=0, tiled=True),
        lax.all_to_all(value_tok, "head", split_axis=1, concat_axis=0, tiled=True),
    )
    local_index = jnp.arange(query_rows, dtype=jnp.int32)
    is_prompt, prompt_index, cont_index, head_pos = row_layout(
        local_index // row_count,
        local_index % row_count,
        block_me,
        heads_axis,
        blocks_axis,
        row_count,
        prompt_dev,
    )
    is_cont = jnp.logical_not(is_prompt)
    local_visible = (
        is_cont[:, None] & is_cont[None, :] & (cont_index[None, :] <= cont_index[:, None])
    )
    queries = query_head.reshape(query_rows, local_heads, DH)
    key_local = key_head.reshape(query_rows, local_heads, DH)
    value_local = value_head.reshape(query_rows, local_heads, DH)
    prompt_keys, prompt_values = (
        lax.all_gather(
            key_head.reshape(heads_axis, row_count, -1)[:, :prompt_dev].reshape(
                heads_axis * prompt_dev, -1
            ),
            "blk",
            axis=0,
            tiled=True,
        ),
        lax.all_gather(
            value_head.reshape(heads_axis, row_count, -1)[:, :prompt_dev].reshape(
                heads_axis * prompt_dev, -1
            ),
            "blk",
            axis=0,
            tiled=True,
        ),
    )
    key_blocks = prompt_keys.reshape(block_count, key_block, local_heads, DH)
    value_blocks = prompt_values.reshape(block_count, key_block, local_heads, DH)
    block_starts = jnp.arange(block_count, dtype=jnp.int32) * key_block
    key_offsets = jnp.arange(key_block, dtype=jnp.int32)

    def prompt_visible(start):
        return is_cont[:, None] | (start + key_offsets[None, :] <= prompt_index[:, None])

    def stats_step(carry, member):
        visible = prompt_visible(member[1])
        return (add_stats(carry, masked_scores(queries, member[0], visible), visible), None)

    start_stats = (
        jnp.full((local_heads, query_rows), NEGATIVE, jnp.float32),
        jnp.zeros((local_heads, query_rows), jnp.float32),
    )
    stats = lax.scan(stats_step, start_stats, (key_blocks, block_starts))[0]
    row_peak, row_total = add_stats(
        stats, masked_scores(queries, key_local, local_visible), local_visible
    )
    log_total = row_peak + jnp.log(row_total)

    def output_step(total_out, member):
        visible = prompt_visible(member[2])
        soft_weights = block_probs(
            masked_scores(queries, member[0], visible), visible, log_total
        ).astype(jnp.bfloat16)
        return (
            total_out
            + jnp.einsum(
                "hqk,khd->qhd", soft_weights, member[1], preferred_element_type=jnp.float32
            ),
            None,
        )

    attn_heads = lax.scan(
        output_step,
        jnp.zeros((query_rows, local_heads, DH), jnp.float32),
        (key_blocks, value_blocks, block_starts),
    )[0]
    local_weights = block_probs(
        masked_scores(queries, key_local, local_visible), local_visible, log_total
    ).astype(jnp.bfloat16)
    attn_heads = attn_heads + jnp.einsum(
        "hqk,khd->qhd", local_weights, value_local, preferred_element_type=jnp.float32
    )
    attn_tok = lax.all_to_all(
        attn_heads.reshape(query_rows, -1).astype(jnp.bfloat16),
        "head",
        split_axis=0,
        concat_axis=1,
        tiled=True,
    )
    residual = tokens + jnp.dot(attn_tok, proj_w, preferred_element_type=jnp.float32)
    hidden_f, second_inverse = norm_rows(residual, second_gain)
    hidden = hidden_f.astype(jnp.bfloat16)
    logits = jnp.einsum("td,ed->te", hidden, router_w, preferred_element_type=jnp.float32)
    soft_route = jax.nn.softmax(logits, axis=-1)
    expert_ids = jnp.arange(EXPERTS, dtype=jnp.int32)
    route_match = routes[:, :, None] == expert_ids[None, None, :]
    gate_values = jnp.sum(jnp.where(route_match, soft_route[:, None, :], 0.0), axis=-1)
    shared_pre = jnp.dot(hidden, shared_w, preferred_element_type=jnp.float32)
    shared_act, shared_slope = swish_parts(shared_pre[:, :SFF])
    shared_up = shared_pre[:, SFF:]
    shared_mid = (shared_act * shared_up).astype(jnp.bfloat16)
    shared_out = jnp.dot(shared_mid, shared_out_w, preferred_element_type=jnp.float32)
    unit_count = expert_w.shape[2]
    per_device = max(1, unit_count // FF)
    spread = max(1, FF // unit_count)
    unit_width = unit_count // per_device
    capacity = max(2, 5 * row_count // (2 * EXPERTS))
    slot_count = blocks_axis * per_device * capacity
    pair_expert = routes.reshape(-1)
    pair_match = route_match.reshape(2 * row_count, EXPERTS).astype(jnp.int32)
    pair_rank = jnp.sum(jnp.cumsum(pair_match, axis=0) * pair_match, axis=1) - 1
    slot_base = (
        pair_expert // per_device * spread * per_device * capacity
        + pair_expert % per_device * capacity
        + pair_rank
    )
    slot_index = (
        slot_base[None, :] + (jnp.arange(spread, dtype=jnp.int32) * per_device * capacity)[:, None]
    )
    pair_ids = jnp.arange(2 * row_count, dtype=jnp.int32)
    slot_pair = (
        jnp.full((slot_count,), 2 * row_count, jnp.int32)
        .at[slot_index.reshape(-1)]
        .set(jnp.tile(pair_ids, spread))
    )
    slot_token = slot_pair // 2
    hidden_pad = jnp.concatenate([hidden, jnp.zeros((1, width_all), jnp.bfloat16)], axis=0)
    send_rows = hidden_pad[slot_token].reshape(blocks_axis, per_device, capacity, width_all)
    received_rows = lax.all_to_all(send_rows, "blk", split_axis=0, concat_axis=0, tiled=True)
    gate_weight = expert_w[0].reshape(width_all, per_device, unit_width)
    up_weight = expert_w[1].reshape(width_all, per_device, unit_width)
    down_w = expert_out_w.reshape(per_device, unit_width, width_all)
    expert_gate = jnp.einsum(
        "tfoa,afw->tfow", received_rows, gate_weight, preferred_element_type=jnp.float32
    )
    expert_up_projection = jnp.einsum(
        "tfoa,afw->tfow", received_rows, up_weight, preferred_element_type=jnp.float32
    )
    expert_activation, expert_slope = swish_parts(expert_gate)
    expert_mid = (expert_activation * expert_up_projection).astype(jnp.bfloat16)
    expert_part = jnp.einsum(
        "secm,emd->secd", expert_mid, down_w, preferred_element_type=jnp.float32
    )
    returned = (
        lax.all_to_all(
            expert_part.astype(jnp.bfloat16), "blk", split_axis=0, concat_axis=0, tiled=True
        )
        .astype(expert_part.dtype)
        .reshape(slot_count, width_all)
    )
    pair_out = jnp.sum(returned[slot_index], axis=0).reshape(row_count, 2, width_all)
    expert_sum = jnp.sum(gate_values[:, :, None] * pair_out, axis=1)
    layer_out = (residual + shared_out + expert_sum).astype(jnp.bfloat16)
    gain_rows, qkv_w, proj_w, router_w, shared_w, shared_out_w, expert_w, expert_out_w = (
        fetch_weights(
            norm_gains,
            attn_qkv,
            attn_proj,
            router_rows,
            shared_gate_up,
            shared_down,
            expert_gate_up,
            expert_down,
        )
    )
    gate_weight = expert_w[0].reshape(width_all, per_device, unit_width)
    up_weight = expert_w[1].reshape(width_all, per_device, unit_width)
    down_w = expert_out_w.reshape(per_device, unit_width, width_all)
    grad_layer = out_grad.astype(jnp.float32)
    grad_smid = jnp.einsum("td,fd->tf", out_grad, shared_out_w, preferred_element_type=jnp.float32)
    shared_grads = jnp.concatenate(
        [grad_smid * shared_up * shared_slope, grad_smid * shared_act], axis=1
    ).astype(jnp.bfloat16)
    grad_hidden = jnp.einsum(
        "tf,df->td", shared_grads, shared_w, preferred_element_type=jnp.float32
    )
    grad_shared_w = jnp.einsum(
        "td,tf->df", hidden, shared_grads, preferred_element_type=jnp.float32
    )
    grad_shared_out = jnp.einsum(
        "tf,td->fd", shared_mid, out_grad, preferred_element_type=jnp.float32
    )
    grad_gates = jnp.sum(grad_layer[:, None, :] * pair_out, axis=-1)
    grad_pairs = (
        (gate_values[:, :, None] * grad_layer[:, None, :])
        .reshape(2 * row_count, width_all)
        .astype(jnp.bfloat16)
    )
    grad_pad = jnp.concatenate([grad_pairs, jnp.zeros((1, width_all), jnp.bfloat16)], axis=0)
    grad_recv = lax.all_to_all(
        grad_pad[slot_pair].reshape(blocks_axis, per_device, capacity, width_all),
        "blk",
        split_axis=0,
        concat_axis=0,
        tiled=True,
    )
    grad_expert_middle = jnp.einsum(
        "secd,emd->secm", grad_recv, down_w, preferred_element_type=jnp.float32
    )
    grad_expert_gate_branch = (grad_expert_middle * expert_up_projection * expert_slope).astype(
        jnp.bfloat16
    )
    grad_expert_up_branch = (grad_expert_middle * expert_activation).astype(jnp.bfloat16)
    grad_rows = jnp.einsum(
        "auwj,buj->auwb", grad_expert_gate_branch, gate_weight, preferred_element_type=jnp.float32
    ) + jnp.einsum(
        "auwj,buj->auwb", grad_expert_up_branch, up_weight, preferred_element_type=jnp.float32
    )
    grad_expert_w = jnp.stack(
        [
            jnp.einsum(
                "jgki,jgkt->igt",
                received_rows,
                grad_expert_gate_branch,
                preferred_element_type=jnp.float32,
            ).reshape(width_all, unit_count),
            jnp.einsum(
                "jgki,jgkt->igt",
                received_rows,
                grad_expert_up_branch,
                preferred_element_type=jnp.float32,
            ).reshape(width_all, unit_count),
        ]
    )
    grad_expert_out = jnp.einsum(
        "secm,secd->emd", expert_mid, grad_recv, preferred_element_type=jnp.float32
    ).reshape(unit_count, width_all)
    grad_back = (
        lax.all_to_all(
            grad_rows.astype(jnp.bfloat16), "blk", split_axis=0, concat_axis=0, tiled=True
        )
        .astype(grad_rows.dtype)
        .reshape(slot_count, width_all)
    )
    grad_hidden = grad_hidden + jnp.sum(
        jnp.sum(grad_back[slot_index], axis=0).reshape(row_count, 2, width_all), axis=1
    )
    grad_soft = jnp.sum(jnp.where(route_match, grad_gates[:, :, None], 0.0), axis=1)
    grad_logits = (
        soft_route * (grad_soft - jnp.sum(soft_route * grad_soft, axis=-1, keepdims=True))
    ).astype(jnp.bfloat16)
    grad_hidden = grad_hidden + jnp.einsum(
        "te,ed->td", grad_logits, router_w, preferred_element_type=jnp.float32
    )
    grad_router = jnp.einsum("te,td->ed", grad_logits, hidden, preferred_element_type=jnp.float32)
    grad_norm_two, grad_second_gain = norm_back(residual, second_inverse, second_gain, grad_hidden)
    grad_resid = grad_layer + grad_norm_two
    grad_branch = grad_resid.astype(jnp.bfloat16)
    grad_proj = jnp.einsum("td,te->de", attn_tok, grad_branch, preferred_element_type=jnp.float32)
    grad_attn_tok = jnp.einsum(
        "te,de->td", grad_branch, proj_w, preferred_element_type=jnp.float32
    ).astype(jnp.bfloat16)
    grad_heads = lax.all_to_all(
        grad_attn_tok, "head", split_axis=1, concat_axis=0, tiled=True
    ).reshape(query_rows, local_heads, DH)
    delta = jnp.transpose(jnp.sum(grad_heads * attn_heads, axis=-1))

    def back_step(grad_acc, member):
        visible = prompt_visible(member[2])
        step_query, step_key, step_value = grad_block(
            queries, grad_heads, log_total, delta, member[0], member[1], visible
        )
        return (grad_acc + step_query, (step_key, step_value))

    grad_query, prompt_grads = lax.scan(
        back_step,
        jnp.zeros((query_rows, local_heads, DH), jnp.float32),
        (key_blocks, value_blocks, block_starts),
    )
    local_query, local_key, local_value = grad_block(
        queries, grad_heads, log_total, delta, key_local, value_local, local_visible
    )
    grad_query = grad_query + local_query
    key_share, value_share = (
        lax.psum_scatter(
            prompt_grads[0].reshape(prompt_all, -1), "blk", scatter_dimension=0, tiled=True
        ),
        lax.psum_scatter(
            prompt_grads[1].reshape(prompt_all, -1), "blk", scatter_dimension=0, tiled=True
        ),
    )
    grad_key = (
        local_key.reshape(heads_axis, row_count, -1)
        .at[:, :prompt_dev]
        .add(key_share.reshape(heads_axis, prompt_dev, -1))
        .reshape(query_rows, local_heads, DH)
    )
    grad_value = (
        local_value.reshape(heads_axis, row_count, -1)
        .at[:, :prompt_dev]
        .add(value_share.reshape(heads_axis, prompt_dev, -1))
    )
    head_cos, head_sin = angle_tables(head_pos)
    grad_query = (
        rotate(grad_query, head_cos, -head_sin).reshape(query_rows, -1).astype(jnp.bfloat16)
    )
    grad_key = rotate(grad_key, head_cos, -head_sin).reshape(query_rows, -1).astype(jnp.bfloat16)
    grad_value = grad_value.reshape(query_rows, -1).astype(jnp.bfloat16)
    grad_q_tok, grad_k_tok, grad_v_tok = (
        lax.all_to_all(grad_query, "head", split_axis=0, concat_axis=1, tiled=True),
        lax.all_to_all(grad_key, "head", split_axis=0, concat_axis=1, tiled=True),
        lax.all_to_all(grad_value, "head", split_axis=0, concat_axis=1, tiled=True),
    )
    grad_qkv_rows = jnp.concatenate([grad_q_tok, grad_k_tok, grad_v_tok], axis=1)
    grad_normed = jnp.einsum("tf,df->td", grad_qkv_rows, qkv_w, preferred_element_type=jnp.float32)
    grad_qkv = jnp.einsum("td,tf->df", normed, grad_qkv_rows, preferred_element_type=jnp.float32)
    grad_norm_one, grad_first_gain = norm_back(tokens, first_inverse, first_gain, grad_normed)
    grad_tokens = grad_resid + grad_norm_one
    owned = (
        lax.psum_scatter(
            jnp.stack([grad_first_gain, grad_second_gain]).astype(jnp.bfloat16),
            ("grp", "head"),
            scatter_dimension=1,
            tiled=True,
        ).astype(jnp.float32),
        lax.psum_scatter(
            grad_qkv.astype(jnp.bfloat16), ("grp", "head"), scatter_dimension=1, tiled=True
        ).astype(jnp.float32),
        lax.psum_scatter(
            grad_proj.astype(jnp.bfloat16), ("grp", "head"), scatter_dimension=1, tiled=True
        ).astype(jnp.float32),
        lax.psum_scatter(
            grad_router.astype(jnp.bfloat16), ("grp", "head"), scatter_dimension=1, tiled=True
        ).astype(jnp.float32),
        lax.psum_scatter(
            grad_shared_w.astype(jnp.bfloat16), ("grp", "head"), scatter_dimension=1, tiled=True
        ).astype(jnp.float32),
        lax.psum_scatter(
            grad_shared_out.astype(jnp.bfloat16), ("grp", "head"), scatter_dimension=1, tiled=True
        ).astype(jnp.float32),
        lax.psum_scatter(
            grad_expert_w.astype(jnp.bfloat16), ("grp", "head"), scatter_dimension=1, tiled=True
        ).astype(jnp.float32),
        lax.psum_scatter(
            grad_expert_out.astype(jnp.bfloat16), ("grp", "head"), scatter_dimension=1, tiled=True
        ).astype(jnp.float32),
    )
    summed = lax.psum((owned[0], owned[1], owned[2], owned[3], owned[4], owned[5]), "blk")
    return (
        layer_out,
        grad_tokens,
        summed[0],
        summed[1],
        summed[2],
        summed[3],
        summed[4],
        summed[5],
        owned[6],
        owned[7],
    )


def solution(mesh):
    placed = (
        P(("grp", "head", "blk"), None),
        P(None, ("grp", "head")),
        P(None, ("grp", "head")),
        P(None, ("grp", "head")),
        P(None, ("grp", "head")),
        P(None, ("grp", "head")),
        P(None, ("grp", "head")),
        P(None, ("grp", "head"), "blk"),
        P("blk", ("grp", "head")),
        P(("grp", "head", "blk"), None),
        P(("grp", "head", "blk"), None),
    )
    return jax.shard_map(
        body,
        mesh=mesh,
        in_specs=placed,
        out_specs=(
            P(("grp", "head", "blk"), None),
            P(("grp", "head", "blk"), None),
            P(None, ("grp", "head")),
            P(None, ("grp", "head")),
            P(None, ("grp", "head")),
            P(None, ("grp", "head")),
            P(None, ("grp", "head")),
            P(None, ("grp", "head")),
            P(None, ("grp", "head"), "blk"),
            P("blk", ("grp", "head")),
        ),
        check_vma=False,
    )
```

profile of v0, /device:TPU:0, one launch (start us, length us, event | category | flops | bytes accessed | tf_op | source)
XLA Modules:
  0.0 1096.6 jit_solution(8065633056595184597)
XLA Ops:
  9.4 6.9 copy.333
  18.9 9.5 all-gather
  34.6 8.3 all-gather.1
  45.1 14.8 %all-gather.9.cloned.1.call-done = bf16[768,2304]{0,1:T(8,128)(2,1)} async-done(((bf16[768,576]{0,1:T(8,128)(2,1)}), bf16[768,2304]{0,1:T(8,128)(2,1)}) %all-gather.9.cloned.1.call-update) | async-done | bytes 3538960 | tf_op jit(solution)/shard_map/all_gather | solution.py:76
  64.1 3.4 all-to-all-start
  69.4 3.5 all-to-all-done
  72.9 3.4 all-to-all-start.1
  76.3 16.3 %all_gather.39 = bf16[1024,384]{1,0:T(8,128)(2,1)S(1)} all-gather(bf16[128,384]{1,0:T(8,128)(2,1)S(1)} %bitcast.414), channel_id=1, replica_groups=mesh['grp'=2,'head'=2,'blk'=8] {'blk'}, dimensions={0}, use_global_device_ids=true | all-gather | bytes 884736 | tf_op jit(solution)/shard_map/all_gather | solution.py:222
  92.6 3.4 all-to-all-start.2
  96.1 15.7 %all_gather.40 = bf16[1024,384]{1,0:T(8,128)(2,1)S(1)} all-gather(bf16[128,384]{1,0:T(8,128)(2,1)S(1)} %bitcast.415), channel_id=1, replica_groups=mesh['grp'=2,'head'=2,'blk'=8] {'blk'}, dimensions={0}, use_global_device_ids=true | all-gather | bytes 884736 | tf_op jit(solution)/shard_map/all_gather | solution.py:214
  117.6 10.6 while.41
  130.2 10.6 while.42
  143.9 3.4 all-to-all-start.3
  148.0 7.3 all-to-all-done.3
  163.2 4.8 all-to-all-start.4
  173.1 9.1 copy.340
  182.2 106.6 %all-gather.17.cloned.1.call-done = bf16[2,768,4096]{2,0,1:T(2,128)(2,1)} async-done(((bf16[2,192,4096]{2,0,1:T(2,128)(2,1)}), bf16[2,768,4096]{2,0,1:T(2,128)(2,1)}) %all-gather.17.cloned.1.call-update) | async-done | bytes 12582928 | tf_op jit(solution)/shard_map/all_gather | solution.py:81
  288.8 29.6 %fusion.154 = (bf16[1,768,4096]{2,0,1:T(2,128)(2,1)}, bf16[1,768,4096]{2,0,1:T(2,128)(2,1)}) fusion(bf16[2,768,4096]{2,0,1:T(2,128)(2,1)} %all-gather.17.cloned.1.call-done), kind=kLoop, calls=%fused_computation.300 | loop fusion | bytes 25165824 | tf_op jit(solution)/shard_map/slice | solution.py:324
  318.4 27.0 %copy.413 = bf16[1,768,4096]{1,2,0:T(8,128)(2,1)} copy(bf16[1,768,4096]{2,0,1:T(2,128)(2,1)} %get-tuple-element.538) | data formatting | bytes 12582912
  345.5 4.6 all-to-all-start.6
  350.1 6.6 fusion.108
  356.7 27.1 %copy.414 = bf16[1,768,4096]{1,2,0:T(8,128)(2,1)} copy(bf16[1,768,4096]{2,0,1:T(2,128)(2,1)} %get-tuple-element.539) | data formatting | bytes 12582912
  383.8 6.9 fusion.106
  390.7 9.2 fusion.83
  402.7 5.7 all-to-all-start.5
  408.4 4.8 fusion.160
  416.0 7.0 all-to-all-done.5
  423.0 4.1 all-to-all-start.7
  427.2 5.3 fusion.159
  432.5 4.6 multiply_convert_fusion.2
  450.9 3.4 multiply_reduce_fusion
  456.2 5.3 convolution_add_fusion.4
  464.5 3.4 all-to-all-start.8
  468.2 5.0 all-to-all-done.8
  475.2 81.4 %while.43 = (s32[]{:T(128)}, f32[256,6,64]{0,2,1:T(8,128)S(1)}, f32[2,512,6,64]{1,0,3,2:T(2,128)}, f32[2,512,6,64]{1,0,3,2:T(2,128)}, bf16[2,512,6,64]{1,3,2,0:T...) while((s32[]{:T(128)}, f32[256,6,64]{0,2,1:T(8,128)S(1)}, ...), condition=%wide.region_25.26_spmd.clone, body=%wide.region_24.25_spmd.clone.sunk | while | flops 513513728 | bytes 40923892 | solution.py:459
  482.3 15.0 %dynamic_update_slice.11 = f32[2,512,6,64]{1,0,3,2:T(2,128)} dynamic-update-slice(f32[2,512,6,64]{1,0,3,2:T(2,128)} %get-tuple-element.824, f32[1,512,6,64]{1,0,3,2:T(1,128)S(1)} %copy.457, s32[]{:T(128)S(6)} %copy.480, s32[]{:T(128)} %constant.215.clone.1..sunk.2, s32[]{:T(128)} %constant.215.clone.1..sunk.2, s32[]{:T(128)} %constant.215.clone.1..sunk.2) | dynamic-update-slice | bytes 1572868 | tf_op jit(solution)/shard_map/while/body/jit(dynamic_update_index_in_dim)/dynamic_update_slice | solution.py:459
  500.9 15.0 %dynamic_update_slice.12 = f32[2,512,6,64]{1,0,3,2:T(2,128)} dynamic-update-slice(f32[2,512,6,64]{1,0,3,2:T(2,128)} %get-tuple-element.825, f32[1,512,6,64]{1,0,3,2:T(1,128)S(1)} %copy.458, s32[]{:T(128)S(6)} %copy.480, s32[]{:T(128)} %constant.215.clone.1..sunk.2, s32[]{:T(128)} %constant.215.clone.1..sunk.2, s32[]{:T(128)} %constant.215.clone.1..sunk.2) | dynamic-update-slice | bytes 1572868 | tf_op jit(solution)/shard_map/while/body/jit(dynamic_update_index_in_dim)/dynamic_update_slice | solution.py:459
  523.0 15.0 %dynamic_update_slice.11 = f32[2,512,6,64]{1,0,3,2:T(2,128)} dynamic-update-slice(f32[2,512,6,64]{1,0,3,2:T(2,128)} %get-tuple-element.824, f32[1,512,6,64]{1,0,3,2:T(1,128)S(1)} %copy.457, s32[]{:T(128)S(6)} %copy.480, s32[]{:T(128)} %constant.215.clone.1..sunk.2, s32[]{:T(128)} %constant.215.clone.1..sunk.2, s32[]{:T(128)} %constant.215.clone.1..sunk.2) | dynamic-update-slice | bytes 1572868 | tf_op jit(solution)/shard_map/while/body/jit(dynamic_update_index_in_dim)/dynamic_update_slice | solution.py:459
  541.6 15.0 %dynamic_update_slice.12 = f32[2,512,6,64]{1,0,3,2:T(2,128)} dynamic-update-slice(f32[2,512,6,64]{1,0,3,2:T(2,128)} %get-tuple-element.825, f32[1,512,6,64]{1,0,3,2:T(1,128)S(1)} %copy.458, s32[]{:T(128)S(6)} %copy.480, s32[]{:T(128)} %constant.215.clone.1..sunk.2, s32[]{:T(128)} %constant.215.clone.1..sunk.2, s32[]{:T(128)} %constant.215.clone.1..sunk.2) | dynamic-update-slice | bytes 1572868 | tf_op jit(solution)/shard_map/while/body/jit(dynamic_update_index_in_dim)/dynamic_update_slice | solution.py:459
  566.0 4.5 convolution_convert_fusion
  580.0 14.0 %reduce-scatter.17.cloned.1.call-done = f32[128,384]{0,1:T(8,128)} async-done(((f32[1024,384]{0,1:T(8,128)}), f32[128,384]{0,1:T(8,128)}) %reduce-scatter.17.cloned.1.call-update) | async-done | bytes 196624 | tf_op jit(solution)/shard_map/reduce_scatter | solution.py:472
  597.0 3.4 all-to-all-start.11
  600.4 28.9 %reduce-scatter.15.cloned.1.call-done = f32[128,384]{0,1:T(8,128)} async-done(((f32[1024,384]{0,1:T(8,128)}), f32[128,384]{0,1:T(8,128)}) %reduce-scatter.15.cloned.1.call-update) | async-done | bytes 196624 | tf_op jit(solution)/shard_map/reduce_scatter | solution.py:469
  630.7 12.6 %scatter-add.6 = f32[2,128,384]{1,0,2:T(2,128)S(1)} dynamic-update-slice(f32[2,128,384]{1,0,2:T(2,128)S(1)} %reshape.950, f32[2,64,384]{1,0,2:T(2,128)S(1)} %copy.365, s32[]{:T(128)} %constant.215.clone.1, s32[]{:T(128)} %constant.215.clone.1, s32[]{:T(128)} %constant.215.clone.1) | dynamic-update-slice | bytes 393220 | tf_op jit(solution)/shard_map/scatter-add | solution.py:479
  644.5 3.4 all-to-all-start.10
  648.7 6.1 all-to-all-done.10
  654.8 3.4 all-to-all-start.9
  658.3 4.7 all-to-all-done.9
  669.8 6.1 bitcast_convert_fusion
  675.9 8.7 copy.378
  686.1 4.6 bitcast_convert_fusion.1
  690.6 8.9 copy.376
  699.5 4.6 bitcast_convert_fusion.2
  704.1 8.5 copy.375
  712.6 10.6 pad_maximum_fusion
  724.4 3.7 fusion.99
  729.0 49.5 %reduce-scatter.23.cloned.1.call-done = bf16[768,1024]{1,0:T(8,128)(2,1)} async-done(((bf16[768,4096]{1,0:T(8,128)(2,1)}), bf16[768,1024]{1,0:T(8,128)(2,1)}) %reduce-scatter.23.cloned.1.call-update) | async-done | bytes 1572880 | tf_op jit(solution)/shard_map/reduce_scatter | solution.py:519
  778.5 31.4 %reduce-scatter.21.cloned.1.call-done = bf16[768,192]{0,1:T(8,128)(2,1)} async-done(((bf16[768,768]{0,1:T(8,128)(2,1)}), bf16[768,192]{0,1:T(8,128)(2,1)}) %reduce-scatter.21.cloned.1.call-update) | async-done | bytes 294928 | tf_op jit(solution)/shard_map/reduce_scatter | solution.py:513
  810.8 26.4 %reduce-scatter.31.cloned.1.call-done = bf16[192,2]{1,0:T(8,128)(2,1)} async-done(((bf16[768,2]{1,0:T(8,128)(2,1)}), bf16[192,2]{1,0:T(8,128)(2,1)}) %reduce-scatter.31.cloned.1.call-update) | async-done | bytes 784
  838.1 49.3 %reduce-scatter.19.cloned.1.call-done = bf16[768,576]{0,1:T(8,128)(2,1)} async-done(((bf16[768,2304]{0,1:T(8,128)(2,1)}), bf16[768,576]{0,1:T(8,128)(2,1)}) %reduce-scatter.19.cloned.1.call-update) | async-done | bytes 884752 | tf_op jit(solution)/shard_map/reduce_scatter | solution.py:510
  887.5 145.3 %all-reduce.4 = (f32[2,192]{1,0:T(2,128)}, f32[768,576]{0,1:T(8,128)}, f32[768,192]{0,1:T(8,128)}, f32[16,192]{1,0:T(8,128)}, f32[768,1024]{1,0:T(8,128)}, /*index=5*/f32[2048,192]{0,1:T(8,128)}) all-reduce(bf16[2,192]{1,0:T(2,128)(2,1)S(1)} %copy.406, ...), channel_id=1, replica_groups=mesh['grp'=2,'head'=2,'blk'=8] {'blk'}, use_global_device_ids=true, to_apply=%region_32.33 | all-reduce | flops 1772928 | bytes 10637568 | tf_op jit(solution)/shard_map/psum | solution.py:532
  1032.8 3.4 convert_element_type.219
  1036.2 48.0 %reduce-scatter.27.cloned.1.call-done = bf16[2,192,4096]{2,1,0:T(8,128)(2,1)} async-done(((bf16[2,768,4096]{2,1,0:T(8,128)(2,1)}), bf16[2,192,4096]{2,1,0:T(8,128)(2,1)}) %reduce-scatter.27.cloned.1.call-update) | async-done | bytes 3145744 | tf_op jit(solution)/shard_map/reduce_scatter | solution.py:525
  1084.2 5.4 convert_element_type.216
  (428 shorter events, 148.7 us)
Async XLA Ops:
  7.2 52.8 %all-gather.9.cloned.1.call-start = ((), (), s32[]{:S(2)}) async-start(), calls=%async_computation.22 | async-start | bytes 4423680 | tf_op jit(solution)/shard_map/all_gather | solution.py:76
  7.9 140.0 %all-gather.11.cloned.1.call-start = ((), (), s32[]{:S(2)}) async-start(), calls=%async_computation.23 | async-start | bytes 1474560 | tf_op jit(solution)/shard_map/all_gather | solution.py:77
  8.7 164.4 %all-gather.19.cloned.1.call-start = ((), (), s32[]{:S(2)}) async-start(), calls=%async_computation.27 | async-start | bytes 7864320 | tf_op jit(solution)/shard_map/all_gather | solution.py:82
  9.4 279.4 %all-gather.17.cloned.1.call-start = ((), (), s32[]{:S(2)}) async-start(), calls=%async_computation.26 | async-start | bytes 15728640 | tf_op jit(solution)/shard_map/all_gather | solution.py:81
  16.3 12.8 %copy-start.9 = (bf16[128,768]{1,0:T(8,128)(2,1)S(1)}, bf16[128,768]{1,0:T(8,128)(2,1)}, u32[]{:S(2)}) copy-start(bf16[128,768]{1,0:T(8,128)(2,1)} %param.21) | copy-start | bytes 589828
  16.3 15.9 %copy-start.20 = (bf16[128,768]{1,0:T(8,128)(2,1)S(1)}, bf16[128,768]{1,0:T(8,128)(2,1)}, u32[]{:S(2)}) copy-start(bf16[128,768]{1,0:T(8,128)(2,1)} %param.31) | copy-start | bytes 589828
  16.3 18.3 %copy-start.61 = (bf16[16,192]{1,0:T(8,128)(2,1)S(1)}, bf16[16,192]{1,0:T(8,128)(2,1)}, u32[]{:S(2)}) copy-start(bf16[16,192]{1,0:T(8,128)(2,1)} %param.25) | copy-start | bytes 18436
  16.3 410.9 %all-gather.13.cloned.1.call-start = ((), (), s32[]{:S(2)}) async-start(), calls=%async_computation.24 | async-start | bytes 7864320 | tf_op jit(solution)/shard_map/all_gather | solution.py:79
  16.9 415.6 %all-gather.15.cloned.1.call-start = ((), (), s32[]{:S(2)}) async-start(), calls=%async_computation.25 | async-start | bytes 3932160 | tf_op jit(solution)/shard_map/all_gather | solution.py:80
  18.1 45.1 %copy-start.69 = (f32[32]{0:T(128)}, f32[32]{0:T(128)S(1)}, u32[]{:S(2)}) copy-start(f32[32]{0:T(128)S(1)} %multiply_power_fusion) | copy-start | bytes 388
  29.1 34.2 %copy-start.44 = (f32[768]{0:T(1024)}, f32[768]{0:T(1024)S(1)}, u32[]{:S(2)}) copy-start(f32[768]{0:T(1024)S(1)} %get-tuple-element.475) | copy-start | bytes 9220
  29.8 33.5 %copy-start.64 = (f32[128]{0:T(128)}, f32[128]{0:T(128)S(1)}, u32[]{:S(2)}) copy-start(f32[128]{0:T(128)S(1)} %get-tuple-element.567) | copy-start | bytes 1540
  64.1 8.8 all-to-all-start
  72.9 19.7 %all-to-all-start.1 = ((bf16[128,2,384]{0,2,1:T(8,128)(2,1)}), bf16[128,2,384]{0,2,1:T(8,128)(2,1)S(1)}, u32[]{:S(2)}, u32[]{:S(2)}) async-start(bf16[128,2,384]{0,2,1:T(8,128)(2,1)} %bitcast.6), calls=%async_computation.1 | async-start | bytes 393216 | tf_op jit(solution)/shard_map/all_to_all | solution.py:193
  92.6 24.7 %all-to-all-start.2 = ((bf16[128,2,384]{0,2,1:T(8,128)(2,1)}), bf16[128,2,384]{0,2,1:T(8,128)(2,1)S(1)}, u32[]{:S(2)}, u32[]{:S(2)}) async-start(bf16[128,2,384]{0,2,1:T(8,128)(2,1)} %bitcast.10), calls=%async_computation.2 | async-start | bytes 393216 | tf_op jit(solution)/shard_map/all_to_all | solution.py:192
  129.8 11.1 %copy-start.2 = (f32[6,256,256]{1,2,0:T(8,128)}, f32[6,256,256]{1,2,0:T(8,128)S(1)}, u32[]{:S(2)}) copy-start(f32[6,256,256]{1,2,0:T(8,128)S(1)} %get-tuple-element.571) | copy-start | bytes 4718596
  130.2 10.6 copy-start.35
  140.8 6.6 copy-start.68
  140.8 14.4 %copy-start.10 = (bf16[128,768]{1,0:T(8,128)(2,1)S(1)}, bf16[128,768]{1,0:T(8,128)(2,1)}, u32[]{:S(2)}) copy-start(bf16[128,768]{1,0:T(8,128)(2,1)} %param.21) | copy-start | bytes 589828
  140.8 17.0 %copy-start.46 = (f32[768]{0:T(1024)S(1)}, f32[768]{0:T(1024)}, u32[]{:S(2)}) copy-start(f32[768]{0:T(1024)} %get-tuple-element.474) | copy-start | bytes 9220
  140.9 16.9 %copy-start.55 = (s32[1024]{0:T(1024)S(1)}, s32[1024]{0:T(1024)}, u32[]{:S(2)}) copy-start(s32[1024]{0:T(1024)} %get-tuple-element.581) | copy-start | bytes 12292
  143.9 11.3 %all-to-all-start.3 = ((bf16[2,128,384]{1,2,0:T(8,128)(2,1)}), bf16[2,128,384]{1,2,0:T(8,128)(2,1)S(1)}, u32[]{:S(2)}, u32[]{:S(2)}) async-start(bf16[2,128,384]{1,2,0:T(8,128)(2,1)} %copy.325), calls=%async_computation.3 | async-start | bytes 393216 | tf_op jit(solution)/shard_map/all_to_all | solution.py:277
  157.8 10.2 copy-start.7
  157.9 10.2 copy-start.42
  157.9 10.4 copy-start.57
  157.9 11.6 %copy-start.23 = (f32[256,768]{1,0:T(8,128)S(1)}, f32[256,768]{1,0:T(8,128)}, u32[]{:S(2)}) copy-start(f32[256,768]{1,0:T(8,128)} %mul.578) | copy-start | bytes 2359300
  160.1 9.6 copy-start.54
  163.2 182.3 %all-to-all-start.4 = ((bf16[8,2,20,768]{3,1,2,0:T(2,128)(2,1)}), bf16[8,2,20,768]{3,1,2,0:T(2,128)(2,1)S(1)}, u32[]{:S(2)}, u32[]{:S(2)}) async-start(bf16[8,2,20,768]{3,1,2,0:T(2,128)(2,1)} %copy.332), calls=%async_computation.4 | async-start | bytes 983040 | tf_op jit(solution)/shard_map/all_to_all | solution.py:323
  345.5 11.2 %copy-start.15 = (bf16[8,2,20,768]{3,1,2,0:T(2,128)(2,1)}, bf16[8,2,20,768]{3,1,2,0:T(2,128)(2,1)S(1)}, u32[]{:S(2)}) copy-start(bf16[8,2,20,768]{3,1,2,0:T(2,128)(2,1)S(1)} %all-to-all-done.4) | copy-start | bytes 1474564
  345.5 45.3 %all-to-all-start.6 = ((bf16[8,2,20,768]{3,1,2,0:T(2,128)(2,1)}), bf16[8,2,20,768]{3,1,2,0:T(2,128)(2,1)}, u32[]{:S(2)}, u32[]{:S(2)}) async-start(bf16[8,2,20,768]{3,1,2,0:T(2,128)(2,1)} %copy.346), calls=%async_computation.6 | async-start | bytes 983040 | tf_op jit(solution)/shard_map/all_to_all | solution.py:384
  383.8 16.1 %slice-start.2 = ((s8[6291456]{0:T(1024)(128)(4,1)}), s8[2097152]{0:T(1024)(128)(4,1)S(1)}, s32[]{:S(2)}) async-start(s8[6291456]{0:T(1024)(128)(4,1)} %bitcast.381), calls=%async_computation.40 | async-start | bytes 4194304
  390.7 9.2 slice-start.3
  402.7 10.5 slice-start
  402.7 20.4 %all-to-all-start.5 = ((bf16[8,2,20,768]{3,1,2,0:T(2,128)(2,1)}), bf16[8,2,20,768]{3,1,2,0:T(2,128)(2,1)}, u32[]{:S(2)}, u32[]{:S(2)}) async-start(bf16[8,2,20,768]{3,1,2,0:T(2,128)(2,1)} %copy.341), calls=%async_computation.5 | async-start | bytes 983040 | tf_op jit(solution)/shard_map/all_to_all | solution.py:339
  423.0 20.4 %all-to-all-start.7 = ((bf16[8,2,20,768]{3,1,2,0:T(2,128)(2,1)}), bf16[8,2,20,768]{3,1,2,0:T(2,128)(2,1)}, u32[]{:S(2)}, u32[]{:S(2)}) async-start(bf16[8,2,20,768]{3,1,2,0:T(2,128)(2,1)} %copy.350), calls=%async_computation.7 | async-start | bytes 983040 | tf_op jit(solution)/shard_map/all_to_all | solution.py:423
  449.2 7.0 copy-start.24
  454.4 7.1 copy-start.48
  456.2 5.3 copy-start.47
  456.2 5.3 copy-start.67
  456.2 6.2 copy-start.73
  456.2 7.1 copy-start.17
  461.5 12.7 %copy-start.33 = (f32[256,6,64]{0,2,1:T(8,128)S(1)}, f32[256,6,64]{0,2,1:T(8,128)}, u32[]{:S(2)}) copy-start(f32[256,6,64]{0,2,1:T(8,128)} %get-tuple-element.573) | copy-start | bytes 1179652
  464.5 8.7 all-to-all-start.8
  467.9 126.0 %reduce-scatter.17.cloned.1.call-start = ((), (), s32[]{:S(2)}) async-start(), calls=%async_computation.29 | async-start | bytes 1769472 | tf_op jit(solution)/shard_map/reduce_scatter | solution.py:472
  559.7 69.7 %reduce-scatter.15.cloned.1.call-start = ((), (), s32[]{:S(2)}) async-start(), calls=%async_computation.28 | async-start | bytes 1769472 | tf_op jit(solution)/shard_map/reduce_scatter | solution.py:469
  561.2 162.1 %reduce-scatter.25.cloned.1.call-start = ((), (), s32[]{:S(2)}) async-start(), calls=%async_computation.33 | async-start | bytes 3932160 | tf_op jit(solution)/shard_map/reduce_scatter | solution.py:522
  564.0 164.1 %reduce-scatter.33.cloned.1.call-start = ((), (), s32[]{:S(2)}) async-start(), calls=%async_computation.37 | async-start | bytes 245760
  565.9 212.6 %reduce-scatter.23.cloned.1.call-start = ((), (), s32[]{:S(2)}) async-start(), calls=%async_computation.32 | async-start | bytes 7864320 | tf_op jit(solution)/shard_map/reduce_scatter | solution.py:519
  570.6 239.3 %reduce-scatter.21.cloned.1.call-start = ((), (), s32[]{:S(2)}) async-start(), calls=%async_computation.31 | async-start | bytes 1474560 | tf_op jit(solution)/shard_map/reduce_scatter | solution.py:513
  578.1 17.0 %copy-start.36 = (f32[2,64,384]{2,1,0:T(8,128)S(1)}, f32[2,64,384]{2,1,0:T(8,128)}, u32[]{:S(2)}) copy-start(f32[2,64,384]{2,1,0:T(8,128)} %copy.416) | copy-start | bytes 589828
  597.0 47.5 %all-to-all-start.11 = ((bf16[2,128,384]{1,2,0:T(8,128)(2,1)}), bf16[2,128,384]{1,2,0:T(8,128)(2,1)S(1)}, u32[]{:S(2)}, u32[]{:S(2)}) async-start(bf16[2,128,384]{1,2,0:T(8,128)(2,1)} %scatter-add.9), calls=%async_computation.13 | async-start | bytes 393216 | tf_op jit(solution)/shard_map/all_to_all | solution.py:496
  630.5 27.9 %copy-start.60 = (bf16[768]{0:T(1024)(128)(2,1)S(1)}, bf16[768]{0:T(1024)(128)(2,1)}, u32[]{:S(2)}) copy-start(bf16[768]{0:T(1024)(128)(2,1)} %get-tuple-element.468) | copy-start | bytes 4612
  630.5 32.6 %copy-start.11 = (bf16[128,768]{1,0:T(8,128)(2,1)S(1)}, bf16[128,768]{1,0:T(8,128)(2,1)}, u32[]{:S(2)}) copy-start(bf16[128,768]{1,0:T(8,128)(2,1)} %param.21) | copy-start | bytes 589828
  630.5 32.6 %copy-start.45 = (f32[768]{0:T(1024)S(1)}, f32[768]{0:T(1024)}, u32[]{:S(2)}) copy-start(f32[768]{0:T(1024)} %copy-done.44) | copy-start | bytes 9220
  630.5 32.6 %copy-start.65 = (f32[128]{0:T(128)S(1)}, f32[128]{0:T(128)}, u32[]{:S(2)}) copy-start(f32[128]{0:T(128)} %copy-done.64) | copy-start | bytes 1540
  644.5 10.3 all-to-all-start.10
  654.8 8.2 all-to-all-start.9
  658.3 179.0 %reduce-scatter.31.cloned.1.call-start = ((), (), s32[]{:S(2)}) async-start(), calls=%async_computation.36 | async-start | bytes 245760
  666.8 220.7 %reduce-scatter.19.cloned.1.call-start = ((), (), s32[]{:S(2)}) async-start(), calls=%async_computation.30 | async-start | bytes 4423680 | tf_op jit(solution)/shard_map/reduce_scatter | solution.py:510
  669.7 363.1 %reduce-scatter.29.cloned.1.call-start = ((), (), s32[]{:S(2)}) async-start(), calls=%async_computation.35 | async-start | bytes 7864320 | tf_op jit(solution)/shard_map/reduce_scatter | solution.py:528
  684.6 399.6 %reduce-scatter.27.cloned.1.call-start = ((), (), s32[]{:S(2)}) async-start(), calls=%async_computation.34 | async-start | bytes 15728640 | tf_op jit(solution)/shard_map/reduce_scatter | solution.py:525
  690.6 8.9 copy-start.6
  723.3 86.6 %copy-start.14 = (f32[128,768]{1,0:T(8,128)S(1)}, f32[128,768]{1,0:T(8,128)}, u32[]{:S(2)}) copy-start(f32[128,768]{1,0:T(8,128)} %copy-done.12) | copy-start | bytes 1179652
  723.3 86.6 %copy-start.72 = (f32[128]{0:T(128)S(1)}, f32[128]{0:T(128)}, u32[]{:S(2)}) copy-start(f32[128]{0:T(128)} %get-tuple-element.566) | copy-start | bytes 1540
  (47 other events, 121.3 us)
Sparse Core Ops, SparseCore 0:
  9.9 50.0 all-gather.8
  61.8 27.9 all-gather.10
  91.7 72.2 all-gather.18
  166.2 122.5 all-gather.16
  290.5 70.1 all-gather.12
  362.4 43.9 all-gather.14
  559.8 34.1 reduce-scatter.16
  596.9 32.4 reduce-scatter.14
  632.9 45.1 reduce-scatter.24
  680.7 23.9 reduce-scatter.32
  708.3 70.2 reduce-scatter.22
  781.3 28.5 reduce-scatter.20
  813.2 23.9 reduce-scatter.30
  840.2 47.2 reduce-scatter.18
  890.3 70.1 reduce-scatter.28
  963.5 120.7 reduce-scatter.26
where the time goes:
time: 1110 us; the launch traced here: 1100 us
  waiting for transfers between devices  406 us (37%)
  local copies, waits for them, and re-layouts  272 us (25%)
  blocking collectives  195 us (18%)
  matrix products  116 us (10%)
  starting transfers between devices  48 us (4%)
  other arithmetic  43.9 us (4%)
  between operations  15.7 us (1%)
    psum x1, blocking collectives, body(): lax.psum((owned[0], owned[1], owned[2], owned[3], owned[4], owned[5]), 'b...  145 us
    all_gather x1, waiting for transfers between devices, fetch_weights(): lax.all_gather(expert_gate_up, ('grp', 'head'), axis=1, tiled=True)  107 us
    unnamed x166, local copies, waits for them, and re-layouts  78.6 us
    dynamic_update_slice x8, local copies, waits for them, and re-layouts, body(): lax.scan(back_step, jnp.zeros((query_rows, local_heads, DH), jnp.float32)...  63.2 us
    reduce_scatter x1, waiting for transfers between devices, body(): lax.psum_scatter(grad_shared_w.astype(jnp.bfloat16), ('grp', 'head'), sca...  49.5 us
    reduce_scatter x1, waiting for transfers between devices, body(): lax.psum_scatter(grad_qkv.astype(jnp.bfloat16), ('grp', 'head'), scatter_...  49.3 us
    reduce_scatter x1, waiting for transfers between devices, body(): lax.psum_scatter(grad_expert_w.astype(jnp.bfloat16), ('grp', 'head'), sca...  48 us
    reduce_scatter x1, waiting for transfers between devices, body(): lax.psum_scatter(grad_proj.astype(jnp.bfloat16), ('grp', 'head'), scatter...  31.4 us
  transfers between devices with their start and end apart: 28, of which 15 were waited for; matrix products, arithmetic and copies ran while one was open for 29% of the time, Pallas kernels for 0%

commit v1 on v0

--- a/solution.py
+++ b/solution.py
@@ -1,6 +1,8 @@
 import jax
 import jax.numpy as jnp
 from jax import lax
+from jax.experimental import pallas as pl
+from jax.experimental.pallas import tpu as pltpu
 from jax.sharding import PartitionSpec as P
 
 HEADS = 12
@@ -544,35 +546,549 @@
     )
 
 
+TRANSPOSED = (((1,), (1,)), ((), ()))
+PLAIN = (((1,), (0,)), ((), ()))
+FIRST = (((0,), (0,)), ((), ()))
+KERNEL_VMEM = 56 * 1024 * 1024
+
+
+def mm(left, right, dims=PLAIN):
+    return lax.dot_general(left, right, dims, preferred_element_type=jnp.float32)
+
+
+def assemble(rows_ref, cut, parts, prompt_to, cont_to):
+    sources = rows_ref.shape[0]
+    blocks = sources // 2
+    half = rows_ref.shape[1]
+    for head_part in range(2):
+        for block in range(blocks):
+            piece = rows_ref[head_part * blocks + block]
+            place = (block * 2 + head_part) * half
+            for order in range(parts):
+                prompt_to[order][place : place + half, :] = piece[
+                    :, order * cut : (order + 1) * cut
+                ]
+                cont_to[order][place : place + half, :] = piece[
+                    :, (parts + order) * cut : (parts + order + 1) * cut
+                ]
+
+
+def spread_out(target, prompt_parts, cont_parts, cut):
+    sources = target.shape[0]
+    blocks = sources // 2
+    half = target.shape[1]
+    for head_part in range(2):
+        for block in range(blocks):
+            place = (block * 2 + head_part) * half
+            pieces = [part[place : place + half, :] for part in prompt_parts]
+            pieces += [part[place : place + half, :] for part in cont_parts]
+            target[head_part * blocks + block] = jnp.concatenate(pieces, axis=1).astype(
+                target.dtype
+            )
+
+
+def causal_mask(rows):
+    keys = lax.broadcasted_iota(jnp.int32, (rows, rows), 0)
+    query = lax.broadcasted_iota(jnp.int32, (rows, rows), 1)
+    return keys <= query
+
+
+def cont_mask(rows, cont):
+    keys = lax.broadcasted_iota(jnp.int32, (rows, rows), 0)
+    query = lax.broadcasted_iota(jnp.int32, (rows, rows), 1)
+    return (keys // cont == query // cont) & (keys <= query)
+
+
+def attention_parts(step, block):
+    if step is None:
+        return None
+    return (0, step * block)
+
+
+def masked_block(keys, queries, mask):
+    scores = mm(keys, queries, TRANSPOSED) * DH ** (-0.5)
+    if mask is None:
+        return scores
+    return jnp.where(mask, scores, NEGATIVE)
+
+
+def attention_kernel(rows_ref, out_ref, qp, kp, vp, qc, kc, vc, op, oc):
+    block = 256
+    prompt = qp.shape[0]
+    assemble(rows_ref, DH, 3, (qp, kp, vp), (qc, kc, vc))
+    cont = 2 * rows_ref.shape[1]
+    for is_cont in range(2):
+        source_q, source_k, source_v, result = (
+            (qc, kc, vc, oc) if is_cont else (qp, kp, vp, op)
+        )
+        mask = cont_mask(block, cont) if is_cont else causal_mask(block)
+        for step in range(prompt // block):
+            rows = slice(step * block, (step + 1) * block)
+            queries = source_q[rows, :]
+            own = masked_block(source_k[rows, :], queries, mask)
+            seen = prompt if is_cont else step * block
+            peak = jnp.max(own, axis=0, keepdims=True)
+            if seen:
+                past = masked_block(kp[0:seen, :], queries, None)
+                peak = jnp.maximum(peak, jnp.max(past, axis=0, keepdims=True))
+            own = jnp.exp(own - peak)
+            total = jnp.sum(own, axis=0, keepdims=True)
+            gathered = mm(source_v[rows, :], own.astype(jnp.bfloat16), FIRST)
+            if seen:
+                past = jnp.exp(past - peak)
+                total = total + jnp.sum(past, axis=0, keepdims=True)
+                gathered = gathered + mm(vp[0:seen, :], past.astype(jnp.bfloat16), FIRST)
+            result[rows, :] = jnp.transpose(gathered / total)
+    spread_out(out_ref, (op,), (oc,), DH)
+
+
+def attention_forward(rows):
+    sources, half, _ = rows.shape
+    prompt = sources * half
+    small = pltpu.VMEM((prompt, DH), jnp.bfloat16)
+    wide = pltpu.VMEM((prompt, DH), jnp.float32)
+    return pl.pallas_call(
+        attention_kernel,
+        out_shape=jax.ShapeDtypeStruct((sources, half, 2 * DH), jnp.bfloat16),
+        in_specs=[pl.BlockSpec(memory_space=pltpu.VMEM)],
+        out_specs=pl.BlockSpec(memory_space=pltpu.VMEM),
+        scratch_shapes=[small] * 6 + [wide] * 2,
+        compiler_params=pltpu.CompilerParams(vmem_limit_bytes=KERNEL_VMEM),
+        cost_estimate=pl.CostEstimate(
+            flops=4 * 2 * prompt * prompt * DH, bytes_accessed=4 * 2**20, transcendentals=2**21
+        ),
+        name="attention_forward",
+    )(rows)
+
+
+def turn_back(values, cosine, sine):
+    half = DH // 2
+    first, second = values[:, :half], values[:, half:]
+    return jnp.concatenate(
+        [first * cosine + second * sine, second * cosine - first * sine], axis=1
+    )
+
+
+def attention_back_kernel(
+    rows_ref, grad_ref, cos_ref, sin_ref, out_ref,
+    qp, kp, vp, qc, kc, vc, gp, gc, dqp, dkp, dvp, dqc, dkc, dvc,
+):
+    block = 256
+    prompt = qp.shape[0]
+    scale = DH ** (-0.5)
+    assemble(rows_ref, DH, 3, (qp, kp, vp), (qc, kc, vc))
+    assemble(grad_ref, DH, 1, (gp,), (gc,))
+    cont = 2 * rows_ref.shape[1]
+    dkp[...] = jnp.zeros_like(dkp)
+    dvp[...] = jnp.zeros_like(dvp)
+    for is_cont in range(2):
+        source_q, source_k, source_v, source_g = (
+            (qc, kc, vc, gc) if is_cont else (qp, kp, vp, gp)
+        )
+        to_q, to_k, to_v = (dqc, dkc, dvc) if is_cont else (dqp, dkp, dvp)
+        mask = cont_mask(block, cont) if is_cont else causal_mask(block)
+        for step in range(prompt // block):
+            rows = slice(step * block, (step + 1) * block)
+            queries = source_q[rows, :]
+            grads = source_g[rows, :]
+            own_keys = source_k[rows, :]
+            own = masked_block(own_keys, queries, mask)
+            seen = prompt if is_cont else step * block
+            peak = jnp.max(own, axis=0, keepdims=True)
+            if seen:
+                past = masked_block(kp[0:seen, :], queries, None)
+                peak = jnp.maximum(peak, jnp.max(past, axis=0, keepdims=True))
+            own = jnp.exp(own - peak)
+            total = jnp.sum(own, axis=0, keepdims=True)
+            if seen:
+                past = jnp.exp(past - peak)
+                total = total + jnp.sum(past, axis=0, keepdims=True)
+            inverse = 1.0 / total
+            own = own * inverse
+            own_grad = mm(source_v[rows, :], grads, TRANSPOSED)
+            delta = jnp.sum(own * own_grad, axis=0, keepdims=True)
+            if seen:
+                past = past * inverse
+                past_grad = mm(vp[0:seen, :], grads, TRANSPOSED)
+                delta = delta + jnp.sum(past * past_grad, axis=0, keepdims=True)
+            own_scores = (own * (own_grad - delta)).astype(jnp.bfloat16)
+            own_dv = mm(own.astype(jnp.bfloat16), grads)
+            own_dk = mm(own_scores, queries) * scale
+            turned = mm(own_keys, own_scores, FIRST)
+            if is_cont:
+                to_v[rows, :] = own_dv
+                to_k[rows, :] = own_dk
+            else:
+                to_v[rows, :] += own_dv
+                to_k[rows, :] += own_dk
+            if seen:
+                past_scores = (past * (past_grad - delta)).astype(jnp.bfloat16)
+                dvp[0:seen, :] += mm(past.astype(jnp.bfloat16), grads)
+                dkp[0:seen, :] += mm(past_scores, queries) * scale
+                turned = turned + mm(kp[0:seen, :], past_scores, FIRST)
+            to_q[rows, :] = jnp.transpose(turned) * scale
+    cos_p, sin_p = cos_ref[0:prompt, :], sin_ref[0:prompt, :]
+    dqp[...] = turn_back(dqp[...], cos_p, sin_p)
+    dkp[...] = turn_back(dkp[...], cos_p, sin_p)
+    for step in range(prompt // cont):
+        rows = slice(step * cont, (step + 1) * cont)
+        cos_c, sin_c = cos_ref[prompt : prompt + cont, :], sin_ref[prompt : prompt + cont, :]
+        dqc[rows, :] = turn_back(dqc[rows, :], cos_c, sin_c)
+        dkc[rows, :] = turn_back(dkc[rows, :], cos_c, sin_c)
+    spread_out(out_ref, (dqp, dkp, dvp), (dqc, dkc, dvc), DH)
+
+
+def attention_backward(rows, grads, cosine, sine):
+    sources, half, wide = rows.shape
+    prompt = sources * half
+    small = pltpu.VMEM((prompt, DH), jnp.bfloat16)
+    large = pltpu.VMEM((prompt, DH), jnp.float32)
+    return pl.pallas_call(
+        attention_back_kernel,
+        out_shape=jax.ShapeDtypeStruct((sources, half, wide), jnp.bfloat16),
+        in_specs=[pl.BlockSpec(memory_space=pltpu.VMEM)] * 4,
+        out_specs=pl.BlockSpec(memory_space=pltpu.VMEM),
+        scratch_shapes=[small] * 8 + [large] * 6,
+        compiler_params=pltpu.CompilerParams(vmem_limit_bytes=KERNEL_VMEM),
+        cost_estimate=pl.CostEstimate(
+            flops=10 * 2 * prompt * prompt * DH, bytes_accessed=8 * 2**20, transcendentals=2**21
+        ),
+        name="attention_backward",
+    )(rows, grads, cosine, sine)
+
+
+def exchange(values, axis, mask):
+    return lax.ppermute(values, axis, [(i, i ^ mask) for i in range(lax.axis_size(axis))])
+
+
+def line_sum(values):
+    place = lax.axis_index("blk")
+    rows = values.shape[0]
+    masks = []
+    mask = 2
+    while mask < lax.axis_size("blk"):
+        masks.append(mask)
+        mask *= 2
+    part = values
+    for mask in masks:
+        half = part.shape[0] // 2
+        upper = (place // mask) % 2
+        kept = lax.dynamic_slice_in_dim(part, upper * half, half, 0)
+        given = lax.dynamic_slice_in_dim(part, (1 - upper) * half, half, 0)
+        part = kept + exchange(given.astype(jnp.bfloat16), "blk", mask).astype(jnp.float32)
+    part = part.astype(jnp.bfloat16)
+    for mask in reversed(masks):
+        upper = (place // mask) % 2 == 1
+        other = exchange(part, "blk", mask)
+        part = jnp.concatenate(
+            [jnp.where(upper, other, part), jnp.where(upper, part, other)], axis=0
+        )
+    return part
+
+
+def pair_order(own, other, core):
+    return jnp.where(core == 0, own, other), jnp.where(core == 0, other, own)
+
+
+def quick_body(
+    tokens_in,
+    norm_gains,
+    attn_qkv,
+    attn_proj,
+    router_rows,
+    shared_gate_up,
+    shared_down,
+    expert_gate_up,
+    expert_down,
+    routes,
+    out_grad,
+):
+    quad = ("grp", "head")
+    line = ("head", "blk")
+    blocks = lax.axis_size("blk")
+    rows, width = tokens_in.shape
+    grp, head, blk = lax.axis_index("grp"), lax.axis_index("head"), lax.axis_index("blk")
+    core = blk % 2
+    quarter = width // 4
+    prompt_dev = max(PROMPT_ROWS, PROMPT_LEAST // (2 * blocks))
+    prompt = prompt_dev * 2 * blocks
+    cont = 2 * (rows - prompt_dev)
+    halves = width // 2
+    bf16, f32 = jnp.bfloat16, jnp.float32
+
+    few = jnp.concatenate([norm_gains, router_rows], axis=0)
+    few = jnp.pad(few, ((0, 20 - few.shape[0]), (0, 0)))
+    few = jnp.concatenate([few[5 * i : 5 * i + 5] for i in range(4)], axis=1)
+    few = jnp.pad(few, ((0, 3), (0, 0)))
+    half_rows = lax.dynamic_slice_in_dim(
+        jnp.concatenate([attn_qkv, attn_proj], axis=1), core * halves, halves, 0
+    )
+    own_w = lax.all_gather(jnp.concatenate([half_rows, few], axis=0), quad, axis=0)
+    other_w = exchange(own_w, "blk", 1)
+    few = own_w[:, halves : halves + 5].reshape(4, 5, 4, quarter)
+    few = jnp.transpose(few, (2, 1, 0, 3)).reshape(20, width)
+    gains = few[0:2].astype(f32)
+    router_w = few[2 : 2 + EXPERTS]
+
+    units = expert_gate_up.shape[2] // 4
+    gate_send = jnp.transpose(expert_gate_up[0].reshape(quarter, 4, units), (1, 0, 2))
+    up_send = jnp.transpose(expert_gate_up[1].reshape(quarter, 4, units), (1, 0, 2))
+    down_send = jnp.transpose(expert_down.reshape(4, units, quarter), (0, 2, 1))
+    gate_w = lax.all_to_all(gate_send, quad, 0, 0, tiled=True).reshape(width, units)
+    up_w = lax.all_to_all(up_send, quad, 0, 0, tiled=True).reshape(width, units)
+    down_w = lax.all_to_all(down_send, quad, 0, 0, tiled=True).reshape(width, units)
+
+    span = SFF // 4
+    shared_half = lax.dynamic_slice_in_dim(shared_gate_up, core * span, span, 1)
+    shared_w = lax.all_gather(shared_half, quad, axis=0)
+    down_half = jnp.concatenate(
+        [
+            lax.dynamic_slice_in_dim(shared_down, core * span, span, 0),
+            lax.dynamic_slice_in_dim(shared_down, 2 * span + core * span, span, 0),
+        ],
+        axis=0,
+    )
+    shared_out_w = lax.all_gather(jnp.transpose(down_half), quad, axis=0).reshape(width, 2 * span)
+
+    expert_ids = jnp.arange(EXPERTS, dtype=jnp.int32)
+    match = (routes[:, :, None] == expert_ids).astype(jnp.int32)
+    flat = match.reshape(2 * rows, EXPERTS)
+    rank = (jnp.sum(jnp.cumsum(flat, axis=0) * flat, axis=1) - 1).reshape(rows, 2)
+    capacity = 5 * rows // (2 * EXPERTS)
+    slots = (routes // 2) * (2 * capacity) + (routes % 2 ^ grp) * capacity + rank
+    slot_ids = jnp.arange(2 * capacity * blocks, dtype=jnp.int32)[:, None]
+    pick = ((slot_ids == slots[:, 0]) | (slot_ids == slots[:, 1])).astype(bf16)
+
+    def dispatch(values):
+        sent = mm(pick, values).astype(bf16).reshape(blocks, 2 * capacity, width)
+        got = lax.all_to_all(sent, "blk", 0, 0, tiled=True)
+        kept = got[:, :capacity].reshape(blocks * capacity, width)
+        given = got[:, capacity:].reshape(blocks * capacity, width)
+        mine = jnp.concatenate([kept, exchange(given, "grp", 1)], axis=0)
+        return jnp.concatenate([mine, exchange(mine, "head", 1)], axis=0)
+
+    def bring_back(values):
+        half = values.shape[0] // 2
+        other = exchange(values[half:].astype(bf16), "head", 1)
+        mine = (values[:half] + other.astype(f32)).astype(bf16)
+        kept = mine[: half // 2].reshape(blocks, capacity, width)
+        given = exchange(mine[half // 2 :], "grp", 1).reshape(blocks, capacity, width)
+        got = lax.all_to_all(
+            jnp.concatenate([kept, given], axis=1), "blk", 0, 0, tiled=True
+        ).reshape(2 * capacity * blocks, width)
+        return mm(pick, got, FIRST)
+
+    grad_rows_in = dispatch(out_grad)
+    grad_two = jnp.concatenate([out_grad, exchange(out_grad, "blk", 1)], axis=0)
+
+    tokens = tokens_in.astype(f32)
+    normed_f, first_inverse = norm_rows(tokens, gains[0])
+    normed = normed_f.astype(bf16)
+    normed_own = lax.dynamic_slice_in_dim(normed, core * halves, halves, 1)
+    normed_other = lax.dynamic_slice_in_dim(normed, (1 - core) * halves, halves, 1)
+    third = attn_qkv.shape[1]
+    mixed = jnp.concatenate(
+        [
+            mm(normed_own, own_w[i, :halves, :third]) + mm(normed_other, other_w[i, :halves, :third])
+            for i in range(4)
+        ],
+        axis=1,
+    )
+    token_row = jnp.arange(rows, dtype=jnp.int32)
+    token_pos = row_layout(head, token_row, blk, 2, blocks, rows, prompt_dev)[3]
+    token_cos, token_sin = angle_tables(token_pos)
+    cubes = mixed.reshape(rows, 3, HEADS, DH)
+    query_tok = rotate(cubes[:, 0], token_cos, token_sin)
+    key_tok = rotate(cubes[:, 1], token_cos, token_sin)
+    cubes = jnp.stack([query_tok, key_tok, cubes[:, 2]], axis=1).astype(bf16)
+
+    def to_heads(values):
+        count = values.shape[1]
+        parts = values.reshape(2, prompt_dev, count, HEADS, DH)
+        parts = jnp.transpose(parts, (3, 1, 0, 2, 4)).reshape(
+            2, HEADS // 2, prompt_dev, 2 * count * DH
+        )
+        parts = jnp.pad(parts, ((0, 0), (0, blocks - HEADS // 2), (0, 0), (0, 0)))
+        parts = parts.reshape(2 * blocks, prompt_dev, 2 * count * DH)
+        return lax.all_to_all(parts, line, 0, 0, tiled=True)
+
+    def to_tokens(values, count):
+        got = lax.all_to_all(values, line, 0, 0, tiled=True)
+        got = got.reshape(2, blocks, prompt_dev, 2, count, DH)[:, : HEADS // 2]
+        return jnp.transpose(got, (3, 2, 4, 0, 1, 5)).reshape(rows, count * width)
+
+    head_rows = to_heads(cubes)
+    attn_tok = to_tokens(attention_forward(head_rows), 1)
+
+    attn_own = lax.dynamic_slice_in_dim(attn_tok, core * halves, halves, 1)
+    attn_other = lax.dynamic_slice_in_dim(attn_tok, (1 - core) * halves, halves, 1)
+    residual = tokens + jnp.concatenate(
+        [
+            mm(attn_own, own_w[i, :halves, third:]) + mm(attn_other, other_w[i, :halves, third:])
+            for i in range(4)
+        ],
+        axis=1,
+    )
+    hidden_f, second_inverse = norm_rows(residual, gains[1])
+    hidden = hidden_f.astype(bf16)
+
+    got_rows = dispatch(hidden)
+    soft = jax.nn.softmax(mm(got_rows, router_w, TRANSPOSED), axis=-1)
+    is_mine = (expert_ids == 2 * blk + grp).astype(f32)
+    gate = jnp.sum(soft * is_mine, axis=1, keepdims=True)
+    e_gate = mm(got_rows, gate_w)
+    e_up = mm(got_rows, up_w)
+    e_act, e_slope = swish_parts(e_gate)
+    e_mid_f = e_act * e_up
+    e_mid = e_mid_f.astype(bf16)
+    e_grad = mm(grad_rows_in, down_w)
+    g_gate = jnp.sum(e_mid_f * e_grad, axis=1, keepdims=True)
+    g_mid = e_grad * gate
+    g_egate = (g_mid * e_up * e_slope).astype(bf16)
+    g_eup = (g_mid * e_act).astype(bf16)
+    g_logits = (g_gate * soft * (is_mine - gate)).astype(bf16)
+    g_rows = (
+        mm(g_egate, gate_w, TRANSPOSED) + mm(g_eup, up_w, TRANSPOSED) + mm(g_logits, router_w)
+    )
+    g_hidden = bring_back(g_rows)
+    g_eout = (gate * grad_rows_in.astype(f32)).astype(bf16)
+    expert_sum = bring_back(gate * mm(e_mid, down_w, TRANSPOSED))
+    g_router = mm(g_logits, got_rows, FIRST)
+
+    def units_back(values):
+        got = lax.all_to_all(
+            values.astype(bf16).reshape(4, quarter, units), quad, 0, 0, tiled=True
+        )
+        return got
+
+    g_gate_w = units_back(mm(got_rows, g_egate, FIRST))
+    g_up_w = units_back(mm(got_rows, g_eup, FIRST))
+    g_down_w = units_back(mm(g_eout, e_mid, FIRST))
+    grad_expert_w = jnp.stack(
+        [
+            jnp.transpose(part, (1, 0, 2)).reshape(quarter, 4 * units).astype(f32)
+            for part in (g_gate_w, g_up_w)
+        ]
+    )
+    grad_expert_out = jnp.transpose(g_down_w, (0, 2, 1)).reshape(4 * units, quarter).astype(f32)
+
+    hidden_two = jnp.concatenate([hidden, exchange(hidden, "blk", 1)], axis=0)
+    s_gate = jnp.concatenate([mm(hidden_two, shared_w[0]), mm(hidden_two, shared_w[1])], axis=1)
+    s_up = jnp.concatenate([mm(hidden_two, shared_w[2]), mm(hidden_two, shared_w[3])], axis=1)
+    s_act, s_slope = swish_parts(s_gate)
+    s_mid = (s_act * s_up).astype(bf16)
+
+    def over_cores(values):
+        return values[:rows] + exchange(values[rows:].astype(bf16), "blk", 1).astype(f32)
+
+    shared_out = over_cores(mm(s_mid, shared_out_w, TRANSPOSED))
+    layer_out = (residual + shared_out + expert_sum).astype(bf16)
+    g_smid = mm(grad_two, shared_out_w)
+    g_sgate = (g_smid * s_up * s_slope).astype(bf16)
+    g_sup = (g_smid * s_act).astype(bf16)
+    g_shared = [g_sgate[:, :span], g_sgate[:, span:], g_sup[:, :span], g_sup[:, span:]]
+    g_hidden = g_hidden + over_cores(
+        sum(mm(g_shared[i], shared_w[i], TRANSPOSED) for i in range(4))
+    )
+    g_shared_w = jnp.stack([mm(hidden_two, part, FIRST) for part in g_shared]).astype(bf16)
+    g_shared_w = lax.psum_scatter(g_shared_w, quad, scatter_dimension=0)
+    g_shared_out = mm(grad_two, s_mid, FIRST).astype(bf16).reshape(4, quarter, 2 * span)
+    g_shared_out = lax.psum_scatter(g_shared_out, quad, scatter_dimension=0)
+    g_shared_sum = line_sum(
+        jnp.concatenate(
+            [g_shared_w, g_shared_out[:, :span], g_shared_out[:, span:]], axis=0
+        ).astype(f32)
+    )
+    first, second = pair_order(g_shared_sum, exchange(g_shared_sum, "blk", 1), core)
+    grad_shared_w = jnp.concatenate([first[:width], second[:width]], axis=1).astype(f32)
+    low_part, high_part = first[width:], second[width:]
+    grad_shared_out = jnp.transpose(
+        jnp.concatenate(
+            [low_part[:quarter], high_part[:quarter], low_part[quarter:], high_part[quarter:]],
+            axis=1,
+        )
+    ).astype(f32)
+
+    g_norm_two, g_second_gain = norm_back(residual, second_inverse, gains[1], g_hidden)
+    g_resid = out_grad.astype(f32) + g_norm_two
+    g_branch = g_resid.astype(bf16)
+    g_branch_parts = [g_branch[:, i * quarter : (i + 1) * quarter] for i in range(4)]
+    g_attn_own = sum(mm(g_branch_parts[i], own_w[i, :halves, third:], TRANSPOSED) for i in range(4))
+    g_attn_other = sum(
+        mm(g_branch_parts[i], other_w[i, :halves, third:], TRANSPOSED) for i in range(4)
+    )
+    g_attn = jnp.concatenate(pair_order(g_attn_own, g_attn_other, core), axis=1).astype(bf16)
+    grad_heads = to_heads(g_attn.reshape(rows, 1, HEADS, DH))
+    all_cos, all_sin = angle_tables(jnp.arange(prompt + cont, dtype=jnp.int32))
+    g_head_rows = attention_backward(head_rows, grad_heads, all_cos[:, 0], all_sin[:, 0])
+    g_qkv = to_tokens(g_head_rows, 3)
+
+    g_qkv_parts = [g_qkv[:, i * third : (i + 1) * third] for i in range(4)]
+    g_normed_own = sum(mm(g_qkv_parts[i], own_w[i, :halves, :third], TRANSPOSED) for i in range(4))
+    g_normed_other = sum(
+        mm(g_qkv_parts[i], other_w[i, :halves, :third], TRANSPOSED) for i in range(4)
+    )
+    g_normed = jnp.concatenate(pair_order(g_normed_own, g_normed_other, core), axis=1)
+    g_norm_one, g_first_gain = norm_back(tokens, first_inverse, gains[0], g_normed)
+    grad_tokens = g_resid + g_norm_one
+
+    def both_cores(own, whole):
+        mine = lax.dynamic_slice_in_dim(own, core * halves, halves, 1)
+        theirs = exchange(lax.dynamic_slice_in_dim(own, (1 - core) * halves, halves, 1), "blk", 1)
+        return mm(mine, whole, FIRST) + mm(theirs, exchange(whole, "blk", 1), FIRST)
+
+    g_qkv_half = both_cores(normed, g_qkv)
+    g_proj_half = both_cores(attn_tok, g_branch)
+    few = jnp.concatenate([g_first_gain[None], g_second_gain[None], g_router], axis=0)
+    few = few + exchange(few, "blk", 1)
+    few = jnp.transpose(
+        jnp.pad(few, ((0, 2), (0, 0))).reshape(4, 5, 4, quarter), (2, 1, 0, 3)
+    ).reshape(4, 5, width)
+    few = jnp.pad(few, ((0, 0), (0, 3), (0, 0)))
+    halved = jnp.concatenate(
+        [
+            jnp.transpose(g_qkv_half.reshape(halves, 4, third), (1, 0, 2)),
+            jnp.transpose(g_proj_half.reshape(halves, 4, quarter), (1, 0, 2)),
+        ],
+        axis=2,
+    )
+    halved = jnp.concatenate([halved, few], axis=1).astype(bf16)
+    halved = lax.psum_scatter(halved, quad, scatter_dimension=0)
+    halved = jnp.pad(halved.astype(f32), ((0, 8), (0, 0)))
+    halved = line_sum(halved)
+    first, second = pair_order(halved, exchange(halved, "blk", 1), core)
+    both = jnp.concatenate([first[:halves], second[:halves]], axis=0).astype(f32)
+    few = first[halves : halves + 5].reshape(5, 4, quarter)
+    few = jnp.transpose(few, (1, 0, 2)).reshape(20, quarter).astype(f32)
+    return (
+        layer_out,
+        grad_tokens,
+        few[0:2],
+        both[:, :third],
+        both[:, third:],
+        few[2 : 2 + EXPERTS],
+        grad_shared_w,
+        grad_shared_out,
+        grad_expert_w,
+        grad_expert_out,
+    )
+
+
 def solution(mesh):
-    placed = (
-        P(("grp", "head", "blk"), None),
-        P(None, ("grp", "head")),
-        P(None, ("grp", "head")),
-        P(None, ("grp", "head")),
-        P(None, ("grp", "head")),
-        P(None, ("grp", "head")),
-        P(None, ("grp", "head")),
-        P(None, ("grp", "head"), "blk"),
-        P("blk", ("grp", "head")),
-        P(("grp", "head", "blk"), None),
-        P(("grp", "head", "blk"), None),
-    )
+    whole = P(("grp", "head", "blk"), None)
+    split = P(None, ("grp", "head"))
+    sizes = dict(mesh.shape)
+    quick = sizes["grp"] == 2 and sizes["head"] == 2 and sizes["blk"] * 2 == EXPERTS
     return jax.shard_map(
-        body,
+        quick_body if quick else body,
         mesh=mesh,
-        in_specs=placed,
+        in_specs=(
+            whole, split, split, split, split, split, split,
+            P(None, ("grp", "head"), "blk"), P("blk", ("grp", "head")), whole, whole,
+        ),
         out_specs=(
-            P(("grp", "head", "blk"), None),
-            P(("grp", "head", "blk"), None),
-            P(None, ("grp", "head")),
-            P(None, ("grp", "head")),
-            P(None, ("grp", "head")),
-            P(None, ("grp", "head")),
-            P(None, ("grp", "head")),
-            P(None, ("grp", "head")),
-            P(None, ("grp", "head"), "blk"),
-            P("blk", ("grp", "head")),
+            whole, whole, split, split, split, split, split, split,
+            P(None, ("grp", "head"), "blk"), P("blk", ("grp", "head")),
         ),
         check_vma=False,
     )

time: 1110 us -> 618 us (0.56)
  blocking collectives: 195 us -> 0 us
  waiting for transfers between devices: 406 us -> 229 us
  local copies, waits for them, and re-layouts: 272 us -> 102 us
  starting transfers between devices: 48 us -> 86.4 us
  Pallas kernels: 0 us -> 19.1 us
    reduce_scatter x8 -> x0, waiting for transfers between devices: 221 us -> none  [the longest x1 49.5 us: body(): lax.psum_scatter(grad_shared_w.astype(jnp.bfloat16), ('grp', 'head'), sca...]
    psum x1 -> x0, blocking collectives: 145 us -> none  [body(): lax.psum((owned[0], owned[1], owned[2], owned[3], owned[4], owned[5]), 'b...]
    ppermute x0 -> x28, waiting for transfers between devices: none -> 140 us  [exchange(): lax.ppermute(values, axis, [(i, i ^ mask) for i in range(lax.axis_size(ax...]
    all_gather x6 -> x3, waiting for transfers between devices: 121 us -> 29.1 us  [the longest x1 29.1 us: quick_body(): lax.all_gather(jnp.concatenate([half_rows, few], axis=0), quad, axis=0)]
    dynamic_update_slice x8 -> x0, local copies, waits for them, and re-layouts: 63.2 us -> none  [body(): lax.scan(back_step, jnp.zeros((query_rows, local_heads, DH), jnp.float32)...]
    unnamed x166 -> x193, local copies, waits for them, and re-layouts: 78.6 us -> 19.3 us
    all_gather x4 -> x0, blocking collectives: 49.8 us -> none  [the longest x1 16.3 us: body(): lax.all_gather(value_head.reshape(heads_axis, row_count, -1)[:, :prompt_d...]
    unnamed x18 -> x9, waiting for transfers between devices: 29.7 us -> 0.14 us
  transfers between devices with their start and end apart: 28 -> 48, of which waited for: 15 -> 23; matrix products, arithmetic and copies ran while one was open for 29% -> 39% of each run, Pallas kernels for 0% -> 3%
where the time goes in v1:
time: 618 us; the launch traced here: 609 us
  waiting for transfers between devices  229 us (37%)
  matrix products  106 us (17%)
  local copies, waits for them, and re-layouts  102 us (17%)
  starting transfers between devices  86.4 us (14%)
  other arithmetic  49.6 us (8%)
  Pallas kernels  19.1 us (3%)
  between operations  16.4 us (3%)
    ppermute x28, waiting for transfers between devices, exchange(): lax.ppermute(values, axis, [(i, i ^ mask) for i in range(lax.axis_size(ax...  140 us
    dot_general x67, matrix products, mm(): lax.dot_general(left, right, dims, preferred_element_type=jnp.float32)  106 us
    all_gather x1, waiting for transfers between devices, quick_body(): lax.all_gather(jnp.concatenate([half_rows, few], axis=0), quad, axis=0)  29.1 us
    ppermute x28, starting transfers between devices, exchange(): lax.ppermute(values, axis, [(i, i ^ mask) for i in range(lax.axis_size(ax...  24.4 us
    unnamed x193, local copies, waits for them, and re-layouts  19.3 us
    convert_element_type x4, local copies, waits for them, and re-layouts, quick_body(): jnp.transpose(part, (1, 0, 2)).reshape(quarter, 4 * units).astype(f32)  13.9 us
    all_to_all x3, starting transfers between devices, units_back(): lax.all_to_all(values.astype(bf16).reshape(4, quarter, units), quad, 0, 0...  12.7 us
    pallas_call x1, Pallas kernels, attention_backward(): pl.pallas_call(attention_back_kernel, out_shape=jax.ShapeDtypeStruct((sou...  12.5 us
  transfers between devices with their start and end apart: 48, of which 23 were waited for; matrix products, arithmetic and copies ran while one was open for 39% of the time, Pallas kernels for 3%

profile of v1, /device:TPU:0, one launch (start us, length us, event | category | flops | bytes accessed | tf_op | source)
XLA Modules:
  0.0 608.8 jit_solution(13701080536831246800)
XLA Ops:
  16.3 6.0 all-to-all-start.7
  23.5 29.1 %all-gather.7.cloned.1.call-done = bf16[1568,768]{1,0:T(8,128)(2,1)} async-done(((bf16[392,768]{1,0:T(8,128)(2,1)}), bf16[1568,768]{1,0:T(8,128)(2,1)}) %all-gather.7.cloned.1.call-update) | async-done | bytes 2408464 | tf_op jit(solution)/shard_map/all_gather | solution.py:826
  67.2 3.1 maximum_bitcast_fusion
  70.3 3.8 copy.288
  78.3 5.9 all-to-all-start
  85.0 3.9 fusion.147
  90.2 8.1 %collective-permute-done.7 = bf16[160,768]{1,0:T(8,128)(2,1)S(1)} collective-permute-done((bf16[160,768]{1,0:T(8,128)(2,1)S(1)}, bf16[160,768]{1,0:T(8,128)(2,1)S(1)}, u32[]{:S(2)}, u32[]{:S(2)}) %collective-permute-start.7) | collective-permute-done | bytes 245792 | tf_op jit(solution)/shard_map/ppermute | solution.py:761
  101.1 2.5 all-to-all-done.rows_ref
  104.5 6.7 %attention_forward.1 = bf16[16,64,128]{2,1,0:T(8,128)(2,1)} custom-call(bf16[16,64,384]{2,1,0:T(8,128)(2,1)} %copy-done.48), custom_call_target="tpu_custom_call" | custom-call | flops 536870912 | bytes 4194304 | tf_op jit(solution)/shard_map/attention_forward/pallas_call | solution.py:650
  111.1 4.4 all-to-all-start.1
  116.9 2.9 reshape_squeeze.7
  121.4 2.9 reshape_squeeze.6
  125.9 2.9 reshape.339
  134.7 3.6 all-to-all-start.4
  156.9 5.1 all-to-all-done.4
  162.0 5.0 all-to-all-start.2
  171.7 3.8 multiply_convert_fusion.4
  175.4 6.2 %all-to-all-done.2 = bf16[8,40,768]{2,1,0:T(8,128)(2,1)S(1)} async-done(((bf16[8,40,768]{2,1,0:T(8,128)(2,1)}), bf16[8,40,768]{2,1,0:T(8,128)(2,1)S(1)}, u32[]{:S(2)}, u32[]{:S(2)}) %all-to-all-start.2) | async-done | bytes 491552 | tf_op jit(solution)/shard_map/all_to_all | solution.py:864
  181.6 4.3 all-to-all-start.3
  188.2 2.7 convolution_convert_fusion.3
  191.0 28.0 %collective-permute-done.3 = bf16[160,768]{1,0:T(8,128)(2,1)S(1)} collective-permute-done((bf16[160,768]{1,0:T(8,128)(2,1)S(1)}, bf16[160,768]{1,0:T(8,128)(2,1)S(1)}, u32[]{:S(2)}, u32[]{:S(2)}) %collective-permute-start.3) | collective-permute-done | bytes 245792 | tf_op jit(solution)/shard_map/ppermute | solution.py:761
  222.3 13.0 %collective-permute-done.4 = bf16[320,768]{1,0:T(8,128)(2,1)S(1)} collective-permute-done((bf16[320,768]{1,0:T(8,128)(2,1)S(1)}, bf16[320,768]{1,0:T(8,128)(2,1)S(1)}, u32[]{:S(2)}, u32[]{:S(2)}) %collective-permute-start.4) | collective-permute-done | bytes 491552 | tf_op jit(solution)/shard_map/ppermute | solution.py:761
  235.3 4.3 all-to-all-start.5
  240.2 4.1 fusion.158
  244.3 4.1 fusion.157
  248.4 9.3 %all-to-all-done.5 = bf16[4,192,1024]{2,1,0:T(8,128)(2,1)} async-done(((bf16[4,192,1024]{2,1,0:T(8,128)(2,1)}), bf16[4,192,1024]{2,1,0:T(8,128)(2,1)}, u32[]{:S(2)}, u32[]{:S(2)}) %all-to-all-start.5) | async-done | bytes 1572896 | tf_op jit(solution)/shard_map/all_to_all | solution.py:839
  257.7 6.5 %multiply_reduce_fusion = (f32[640]{0:T(1024)S(1)}, bf16[640,1024]{1,0:T(8,128)(2,1)S(1)}, bf16[640,1024]{1,0:T(8,128)(2,1)S(1)}, bf16[640,1024]{1,0:T(8,128)(2,1)}) fusion(f32[640,1024]{1,0:T(8,128)} %fusion.158, f32[640,1024]{1,0:T(8,128)} %fusion.157, f32[640]{0:T(1024)S(1)} %multiply_reduce_fusion.4, ...), kind=kOutput, calls=%fused_computation.8 | convolution fusion | flops 1018428800 | bytes 11736064 | tf_op jit(solution)/shard_map/dot_general | solution.py:556
  264.2 3.6 fusion.159
  271.9 10.5 %collective-permute-done.9 = bf16[320,768]{1,0:T(8,128)(2,1)S(1)} collective-permute-done((bf16[320,768]{1,0:T(8,128)(2,1)S(1)}, bf16[320,768]{1,0:T(8,128)(2,1)S(1)}, u32[]{:S(2)}, u32[]{:S(2)}) %collective-permute-start.9) | collective-permute-done | bytes 491552 | tf_op jit(solution)/shard_map/ppermute | solution.py:761
  286.3 3.8 collective-permute-done.10
  292.0 4.3 all-to-all-start.8
  301.8 9.2 %all-to-all-done.8 = bf16[8,40,768]{2,1,0:T(8,128)(2,1)} async-done(((bf16[8,40,768]{2,1,0:T(8,128)(2,1)}), bf16[8,40,768]{2,1,0:T(8,128)(2,1)}, u32[]{:S(2)}, u32[]{:S(2)}) %all-to-all-start.8) | async-done | bytes 491552 | tf_op jit(solution)/shard_map/all_to_all | solution.py:876
  324.9 3.5 all-to-all-start.9
  328.5 3.2 multiply_sine_fusion
  331.7 6.9 %all-to-all-done.9.grad_ref = bf16[16,64,128]{2,1,0:T(8,128)(2,1)S(1)} async-done(((bf16[16,64,128]{2,1,0:T(8,128)(2,1)}), bf16[16,64,128]{2,1,0:T(8,128)(2,1)S(1)}, u32[]{:S(2)}, u32[]{:S(2)}) %all-to-all-start.9) | async-done | bytes 262176 | tf_op jit(solution)/shard_map/all_to_all | solution.py:913
  339.3 12.5 %attention_backward.1 = bf16[16,64,384]{2,1,0:T(8,128)(2,1)} custom-call(bf16[16,64,384]{2,1,0:T(8,128)(2,1)} %copy-done.48, bf16[16,64,128]{2,1,0:T(8,128)(2,1)} %copy-done.50, f32[1152,32]{1,0:T(8,128)} %get-tuple-element.118.cos_ref, f32[1152,32]{1,0:T(8,128)} %get-tuple-element.117.sin_ref), custom_call_target="tpu_custom_call" | custom-call | flops 1342177280 | bytes 8388608 | tf_op jit(solution)/shard_map/attention_backward/pallas_call | solution.py:746
  351.8 3.8 all-to-all-start.10
  356.6 3.9 convolution_convert_fusion.1
  363.4 11.5 %all-to-all-done.10 = bf16[16,64,384]{2,1,0:T(8,128)(2,1)S(1)} async-done(((bf16[16,64,384]{2,1,0:T(8,128)(2,1)}), bf16[16,64,384]{2,1,0:T(8,128)(2,1)S(1)}, u32[]{:S(2)}, u32[]{:S(2)}) %all-to-all-start.10) | async-done | bytes 786464 | tf_op jit(solution)/shard_map/all_to_all | solution.py:916
  374.9 4.4 all-to-all-start.12
  379.3 2.5 reshape.352
  383.8 2.9 copy.330
  386.7 2.6 reshape.353
  403.2 2.8 fusion.1
  408.3 3.1 fusion.2
  411.4 4.5 copy.342
  417.2 2.8 convolution_multiply_fusion
  423.7 2.6 convolution_convert_fusion.2
  426.3 4.0 all-to-all-start.11
  435.6 3.9 convolution_convert_fusion
  439.5 15.4 %collective-permute-done.5 = bf16[320,768]{1,0:T(8,128)(2,1)} collective-permute-done((bf16[320,768]{1,0:T(8,128)(2,1)}, bf16[320,768]{1,0:T(8,128)(2,1)}, u32[]{:S(2)}, u32[]{:S(2)}) %collective-permute-start.5) | collective-permute-done | bytes 491552 | tf_op jit(solution)/shard_map/ppermute | solution.py:761
  456.1 9.2 %all-to-all-done.11 = bf16[4,192,1024]{2,1,0:T(8,128)(2,1)S(1)} async-done(((bf16[4,192,1024]{2,1,0:T(8,128)(2,1)}), bf16[4,192,1024]{2,1,0:T(8,128)(2,1)S(1)}, u32[]{:S(2)}, u32[]{:S(2)}) %all-to-all-start.11) | async-done | bytes 1572896 | tf_op jit(solution)/shard_map/all_to_all | solution.py:959
  465.3 4.4 all-to-all-start.13
  480.0 16.6 %collective-permute-done.6 = bf16[160,768]{1,0:T(8,128)(2,1)} collective-permute-done((bf16[160,768]{1,0:T(8,128)(2,1)}, bf16[160,768]{1,0:T(8,128)(2,1)}, u32[]{:S(2)}, u32[]{:S(2)}) %collective-permute-start.6) | collective-permute-done | bytes 245792 | tf_op jit(solution)/shard_map/ppermute | solution.py:761
  500.1 3.8 copy.345
  503.9 3.8 convert_element_type.298
  510.1 3.9 convert_element_type.295
  517.7 3.7 all-to-all-start.6
  521.4 4.5 maximum_convert_fusion
  525.9 11.8 %collective-permute-done.25 = bf16[288,512]{1,0:T(8,128)(2,1)} collective-permute-done((bf16[288,512]{1,0:T(8,128)(2,1)S(1)}, bf16[288,512]{1,0:T(8,128)(2,1)}, u32[]{:S(2)}, u32[]{:S(2)}) %collective-permute-start.25) | collective-permute-done | bytes 294944 | tf_op jit(solution)/shard_map/ppermute | solution.py:761
  548.7 7.4 %collective-permute-done.26 = bf16[576,512]{1,0:T(8,128)(2,1)} collective-permute-done((bf16[576,512]{1,0:T(8,128)(2,1)}, bf16[576,512]{1,0:T(8,128)(2,1)}, u32[]{:S(2)}, u32[]{:S(2)}) %collective-permute-start.26) | collective-permute-done | bytes 589856 | tf_op jit(solution)/shard_map/ppermute | solution.py:761
  562.8 8.8 %collective-permute-done.19 = bf16[100,768]{1,0:T(8,128)(2,1)S(1)} collective-permute-done((bf16[100,768]{1,0:T(8,128)(2,1)S(1)}, bf16[100,768]{1,0:T(8,128)(2,1)S(1)}, u32[]{:S(2)}, u32[]{:S(2)}) %collective-permute-start.19) | collective-permute-done | bytes 153632 | tf_op jit(solution)/shard_map/ppermute | solution.py:761
  573.0 8.3 %collective-permute-done.20 = bf16[100,768]{1,0:T(8,128)(2,1)S(1)} collective-permute-done((bf16[100,768]{1,0:T(8,128)(2,1)S(1)}, bf16[100,768]{1,0:T(8,128)(2,1)S(1)}, u32[]{:S(2)}, u32[]{:S(2)}) %collective-permute-start.20) | collective-permute-done | bytes 153632 | tf_op jit(solution)/shard_map/ppermute | solution.py:761
  583.3 4.9 collective-permute-done.21
  (465 shorter events, 191.1 us)
Async XLA Ops:
  7.2 45.3 %all-gather.7.cloned.1.call-start = ((), (), s32[]{:S(2)}) async-start(), calls=%async_computation.17 | async-start | bytes 3010560 | tf_op jit(solution)/shard_map/all_gather | solution.py:826
  11.8 140.4 %all-gather.9.cloned.1.call-start = ((), (), s32[]{:S(2)}) async-start(), calls=%async_computation.18 | async-start | bytes 3932160 | tf_op jit(solution)/shard_map/all_gather | solution.py:843
  12.8 117.6 %collective-permute-start.11 = (bf16[128,768]{1,0:T(8,128)(2,1)S(1)}, bf16[128,768]{1,0:T(8,128)(2,1)}, u32[]{:S(2)}, u32[]{:S(2)}) collective-permute-start(bf16[128,768]{1,0:T(8,128)(2,1)S(1)} %copy-done.32), channel_id=1, source_target_pairs={{0,1},{1,0},{2,3},{3,2},{4,5},{5,4},{6,7},{7,6},{8,9},{9,8},{10,11... | collective-permute-start | bytes 589832 | tf_op jit(solution)/shard_map/ppermute | solution.py:761
  15.3 135.8 %copy-start.62 = (s32[128]{0:T(128)}, s32[128]{0:T(128)S(1)}, u32[]{:S(2)}) copy-start(s32[128]{0:T(128)S(1)} %get-tuple-element.64) | copy-start | bytes 1540
  15.3 135.8 %copy-start.65 = (s32[128]{0:T(128)}, s32[128]{0:T(128)S(1)}, u32[]{:S(2)}) copy-start(s32[128]{0:T(128)S(1)} %get-tuple-element.65) | copy-start | bytes 1540
  16.3 62.0 %all-to-all-start.7 = ((bf16[8,40,768]{2,1,0:T(8,128)(2,1)}), bf16[8,40,768]{2,1,0:T(8,128)(2,1)S(1)}, u32[]{:S(2)}, u32[]{:S(2)}) async-start(bf16[8,40,768]{2,1,0:T(8,128)(2,1)} %bitcast.34), calls=%async_computation.7 | async-start | bytes 983040 | tf_op jit(solution)/shard_map/all_to_all | solution.py:864
  22.3 149.3 %all-gather.11.cloned.1.call-start = ((), (), s32[]{:S(2)}) async-start(), calls=%async_computation.19 | async-start | bytes 1966080 | tf_op jit(solution)/shard_map/all_gather | solution.py:851
  52.5 8.2 %collective-permute-start = (bf16[4,392,768]{2,1,0:T(8,128)(2,1)}, bf16[4,392,768]{2,1,0:T(8,128)(2,1)}, u32[]{:S(2)}, u32[]{:S(2)}) collective-permute-start(bf16[4,392,768]{2,1,0:T(8,128)(2,1)} %bitcast.240), channel_id=1, source_target_pairs={{0,1},{1,0},{2,3},{3,2},{4,5},{5,4},{6,7},{7,6},{8,9},{9,8},{10,11... | collective-permute-start | bytes 7225352 | tf_op jit(solution)/shard_map/ppermute | solution.py:761
  78.3 25.3 %all-to-all-start = ((bf16[16,64,384]{2,1,0:T(8,128)(2,1)}), bf16[16,64,384]{2,1,0:T(8,128)(2,1)S(1)}, u32[]{:S(2)}, u32[]{:S(2)}) async-start(bf16[16,64,384]{2,1,0:T(8,128)(2,1)} %bitcast.14), calls=%async_computation | async-start | bytes 1572864 | tf_op jit(solution)/shard_map/all_to_all | solution.py:913
  84.4 14.0 %collective-permute-start.7 = (bf16[160,768]{1,0:T(8,128)(2,1)S(1)}, bf16[160,768]{1,0:T(8,128)(2,1)S(1)}, u32[]{:S(2)}, u32[]{:S(2)}) collective-permute-start(bf16[160,768]{1,0:T(8,128)(2,1)S(1)} %reshape.346), channel_id=1, source_target_pairs={{0,16},{16,0},{1,17},{17,1},{2,18},{18,2},{3,19},{19,3},{4,20},{20... | collective-permute-start | bytes 737288 | tf_op jit(solution)/shard_map/ppermute | solution.py:761
  99.2 33.7 %collective-permute-start.8 = (bf16[320,768]{1,0:T(8,128)(2,1)}, bf16[320,768]{1,0:T(8,128)(2,1)}, u32[]{:S(2)}, u32[]{:S(2)}) collective-permute-start(bf16[320,768]{1,0:T(8,128)(2,1)} %pad_maximum_fusion.10), channel_id=1, source_target_pairs={{0,8},{8,0},{1,9},{9,1},{2,10},{10,2},{3,11},{11,3},{4,12},{12,4},... | collective-permute-start | bytes 1474568 | tf_op jit(solution)/shard_map/ppermute | solution.py:761
  111.1 23.6 %all-to-all-start.1 = ((bf16[16,64,128]{2,1,0:T(8,128)(2,1)}), bf16[16,64,128]{2,1,0:T(8,128)(2,1)S(1)}, u32[]{:S(2)}, u32[]{:S(2)}) async-start(bf16[16,64,128]{2,1,0:T(8,128)(2,1)} %attention_forward.1), calls=%async_computation.1 | async-start | bytes 524288 | tf_op jit(solution)/shard_map/all_to_all | solution.py:916
  134.7 27.3 %all-to-all-start.4 = ((bf16[4,192,1024]{2,1,0:T(8,128)(2,1)}), bf16[4,192,1024]{2,1,0:T(8,128)(2,1)S(1)}, u32[]{:S(2)}, u32[]{:S(2)}) async-start(bf16[4,192,1024]{2,1,0:T(8,128)(2,1)} %copy.311), calls=%async_computation.4 | async-start | bytes 3145728 | tf_op jit(solution)/shard_map/all_to_all | solution.py:838
  150.6 1.6 collective-permute-start.1
  152.2 17.2 %copy-start.14 = (bf16[128,768]{0,1:T(8,128)(2,1)}, bf16[128,768]{0,1:T(8,128)(2,1)S(1)}, u32[]{:S(2)}) copy-start(bf16[128,768]{0,1:T(8,128)(2,1)S(1)} %collective-permute-done.1) | copy-start | bytes 589828
  162.0 19.7 %all-to-all-start.2 = ((bf16[8,40,768]{2,1,0:T(8,128)(2,1)}), bf16[8,40,768]{2,1,0:T(8,128)(2,1)S(1)}, u32[]{:S(2)}, u32[]{:S(2)}) async-start(bf16[8,40,768]{2,1,0:T(8,128)(2,1)} %bitcast.26), calls=%async_computation.2 | async-start | bytes 983040 | tf_op jit(solution)/shard_map/all_to_all | solution.py:864
  175.4 45.1 %copy-start.26 = (bf16[256,1024]{1,0:T(8,128)(2,1)}, bf16[256,1024]{1,0:T(8,128)(2,1)S(1)}, u32[]{:S(2)}) copy-start(bf16[256,1024]{1,0:T(8,128)(2,1)S(1)} %get-tuple-element.79) | copy-start | bytes 1572868
  181.6 53.6 %all-to-all-start.3 = ((bf16[4,192,1024]{2,1,0:T(8,128)(2,1)}), bf16[4,192,1024]{2,1,0:T(8,128)(2,1)}, u32[]{:S(2)}, u32[]{:S(2)}) async-start(bf16[4,192,1024]{2,1,0:T(8,128)(2,1)} %copy.310), calls=%async_computation.3 | async-start | bytes 3145728 | tf_op jit(solution)/shard_map/all_to_all | solution.py:837
  186.0 244.3 %reduce-scatter.14.cloned.1.call-start = ((), (), s32[]{:S(2)}) async-start(), calls=%async_computation.22 | async-start | bytes 1966080
  186.2 32.8 %collective-permute-start.3 = (bf16[160,768]{1,0:T(8,128)(2,1)S(1)}, bf16[160,768]{1,0:T(8,128)(2,1)S(1)}, u32[]{:S(2)}, u32[]{:S(2)}) collective-permute-start(bf16[160,768]{1,0:T(8,128)(2,1)S(1)} %reshape.336), channel_id=1, source_target_pairs={{0,16},{16,0},{1,17},{17,1},{2,18},{18,2},{3,19},{19,3},{4,20},{20... | collective-permute-start | bytes 737288 | tf_op jit(solution)/shard_map/ppermute | solution.py:761
  219.0 16.2 %collective-permute-start.4 = (bf16[320,768]{1,0:T(8,128)(2,1)S(1)}, bf16[320,768]{1,0:T(8,128)(2,1)S(1)}, u32[]{:S(2)}, u32[]{:S(2)}) collective-permute-start(bf16[320,768]{1,0:T(8,128)(2,1)S(1)} %pad_maximum_fusion.8), channel_id=1, source_target_pairs={{0,8},{8,0},{1,9},{9,1},{2,10},{10,2},{3,11},{11,3},{4,12},{12,4},... | collective-permute-start | bytes 1474568 | tf_op jit(solution)/shard_map/ppermute | solution.py:761
  222.2 17.4 %copy-start.52 = (bf16[20,768]{1,0:T(8,128)(2,1)S(1)}, bf16[20,768]{1,0:T(8,128)(2,1)}, u32[]{:S(2)}) copy-start(bf16[20,768]{1,0:T(8,128)(2,1)} %copy-done.51) | copy-start | bytes 92164
  235.3 121.3 %copy-start.5 = (bf16[640,768]{1,0:T(8,128)(2,1)}, bf16[640,768]{1,0:T(8,128)(2,1)S(1)}, u32[]{:S(2)}) copy-start(bf16[640,768]{1,0:T(8,128)(2,1)S(1)} %constant_dynamic-update-slice_fusion) | copy-start | bytes 2949124
  235.3 22.4 %all-to-all-start.5 = ((bf16[4,192,1024]{2,1,0:T(8,128)(2,1)}), bf16[4,192,1024]{2,1,0:T(8,128)(2,1)}, u32[]{:S(2)}, u32[]{:S(2)}) async-start(bf16[4,192,1024]{2,1,0:T(8,128)(2,1)} %copy.312), calls=%async_computation.5 | async-start | bytes 3145728 | tf_op jit(solution)/shard_map/all_to_all | solution.py:839
  240.1 29.0 %copy-start.42 = (f32[640,16]{0,1:T(8,128)}, f32[640,16]{0,1:T(8,128)S(1)}, u32[]{:S(2)}) copy-start(f32[640,16]{0,1:T(8,128)S(1)} %get-tuple-element.129) | copy-start | bytes 122884
  240.2 28.9 %copy-start.55 = (f32[640]{0:T(1024)}, f32[640]{0:T(1024)S(1)}, u32[]{:S(2)}) copy-start(f32[640]{0:T(1024)S(1)} %multiply_reduce_fusion.4) | copy-start | bytes 7684
  269.8 12.7 %collective-permute-start.9 = (bf16[320,768]{1,0:T(8,128)(2,1)S(1)}, bf16[320,768]{1,0:T(8,128)(2,1)S(1)}, u32[]{:S(2)}, u32[]{:S(2)}) collective-permute-start(bf16[320,768]{1,0:T(8,128)(2,1)S(1)} %slice.644), channel_id=1, source_target_pairs={{0,8},{8,0},{1,9},{9,1},{2,10},{10,2},{3,11},{11,3},{4,12},{12,4},... | collective-permute-start | bytes 1474568 | tf_op jit(solution)/shard_map/ppermute | solution.py:761
  283.3 6.8 %collective-permute-start.10 = (bf16[160,768]{1,0:T(8,128)(2,1)}, bf16[160,768]{1,0:T(8,128)(2,1)}, u32[]{:S(2)}, u32[]{:S(2)}) collective-permute-start(bf16[160,768]{1,0:T(8,128)(2,1)} %get-tuple-element.96), channel_id=1, source_target_pairs={{0,16},{16,0},{1,17},{17,1},{2,18},{18,2},{3,19},{19,3},{4,20},{20... | collective-permute-start | bytes 737288 | tf_op jit(solution)/shard_map/ppermute | solution.py:761
  286.3 15.5 %collective-permute-start.12 = (bf16[128,768]{0,1:T(8,128)(2,1)}, bf16[128,768]{0,1:T(8,128)(2,1)}, u32[]{:S(2)}, u32[]{:S(2)}) collective-permute-start(bf16[128,768]{0,1:T(8,128)(2,1)} %slice.646), channel_id=1, source_target_pairs={{0,1},{1,0},{2,3},{3,2},{4,5},{5,4},{6,7},{7,6},{8,9},{9,8},{10,11... | collective-permute-start | bytes 589832 | tf_op jit(solution)/shard_map/ppermute | solution.py:761
  292.0 19.0 %all-to-all-start.8 = ((bf16[8,40,768]{2,1,0:T(8,128)(2,1)}), bf16[8,40,768]{2,1,0:T(8,128)(2,1)}, u32[]{:S(2)}, u32[]{:S(2)}) async-start(bf16[8,40,768]{2,1,0:T(8,128)(2,1)} %pad_maximum_fusion.11), calls=%async_computation.8 | async-start | bytes 983040 | tf_op jit(solution)/shard_map/all_to_all | solution.py:876
  296.2 135.2 %reduce-scatter.12.cloned.1.call-start = ((), (), s32[]{:S(2)}) async-start(), calls=%async_computation.21 | async-start | bytes 3932160
  324.9 13.7 %all-to-all-start.9 = ((bf16[16,64,128]{2,1,0:T(8,128)(2,1)}), bf16[16,64,128]{2,1,0:T(8,128)(2,1)S(1)}, u32[]{:S(2)}, u32[]{:S(2)}) async-start(bf16[16,64,128]{2,1,0:T(8,128)(2,1)} %bitcast.37), calls=%async_computation.9 | async-start | bytes 524288 | tf_op jit(solution)/shard_map/all_to_all | solution.py:913
  339.3 16.4 %copy-start.17 = (bf16[128,384]{0,1:T(8,128)(2,1)S(1)}, bf16[128,384]{0,1:T(8,128)(2,1)}, u32[]{:S(2)}) copy-start(bf16[128,384]{0,1:T(8,128)(2,1)} %copy-done.16) | copy-start | bytes 294916
  339.3 16.9 %copy-start.19 = (bf16[128,384]{0,1:T(8,128)(2,1)S(1)}, bf16[128,384]{0,1:T(8,128)(2,1)}, u32[]{:S(2)}) copy-start(bf16[128,384]{0,1:T(8,128)(2,1)} %copy-done.18) | copy-start | bytes 294916
  339.3 17.0 %copy-start.43 = (f32[640,16]{0,1:T(8,128)S(1)}, f32[640,16]{0,1:T(8,128)}, u32[]{:S(2)}) copy-start(f32[640,16]{0,1:T(8,128)} %copy-done.42) | copy-start | bytes 122884
  339.3 17.0 %copy-start.56 = (f32[640]{0:T(1024)S(1)}, f32[640]{0:T(1024)}, u32[]{:S(2)}) copy-start(f32[640]{0:T(1024)} %copy-done.55) | copy-start | bytes 7684
  339.3 17.0 %copy-start.60 = (f32[640]{0:T(1024)S(1)}, f32[640]{0:T(1024)}, u32[]{:S(2)}) copy-start(f32[640]{0:T(1024)} %copy-done.59) | copy-start | bytes 7684
  339.3 17.0 %copy-start.72 = (f32[16]{0:T(128)S(1)}, f32[16]{0:T(128)}, u32[]{:S(2)}) copy-start(f32[16]{0:T(128)} %compare_convert_fusion) | copy-start | bytes 196
  351.8 23.1 %all-to-all-start.10 = ((bf16[16,64,384]{2,1,0:T(8,128)(2,1)}), bf16[16,64,384]{2,1,0:T(8,128)(2,1)S(1)}, u32[]{:S(2)}, u32[]{:S(2)}) async-start(bf16[16,64,384]{2,1,0:T(8,128)(2,1)} %attention_backward.1), calls=%async_computation.10 | async-start | bytes 1572864 | tf_op jit(solution)/shard_map/all_to_all | solution.py:916
  355.7 47.5 %collective-permute-start.13 = (bf16[128,384]{0,1:T(8,128)(2,1)S(1)}, bf16[128,384]{0,1:T(8,128)(2,1)}, u32[]{:S(2)}, u32[]{:S(2)}) collective-permute-start(bf16[128,384]{0,1:T(8,128)(2,1)S(1)} %copy-done.17), channel_id=1, source_target_pairs={{0,1},{1,0},{2,3},{3,2},{4,5},{5,4},{6,7},{7,6},{8,9},{9,8},{10,11... | collective-permute-start | bytes 294920 | tf_op jit(solution)/shard_map/ppermute | solution.py:761
  356.2 5.1 collective-permute-start.15
  360.5 1.5 collective-permute-start.16
  374.9 51.5 %all-to-all-start.12 = ((bf16[4,192,1024]{2,1,0:T(8,128)(2,1)}), bf16[4,192,1024]{2,1,0:T(8,128)(2,1)}, u32[]{:S(2)}, u32[]{:S(2)}) async-start(bf16[4,192,1024]{2,1,0:T(8,128)(2,1)} %bitcast.272), calls=%async_computation.12 | async-start | bytes 3145728 | tf_op jit(solution)/shard_map/all_to_all | solution.py:959
  379.2 166.2 %reduce-scatter.10.cloned.1.call-start = ((), (), s32[]{:S(2)}) async-start(), calls=%async_computation.20 | async-start | bytes 3010560
  389.3 13.9 %collective-permute-start.14 = (bf16[128,2304]{0,1:T(8,128)(2,1)S(1)}, bf16[128,2304]{0,1:T(8,128)(2,1)}, u32[]{:S(2)}, u32[]{:S(2)}) collective-permute-start(bf16[128,2304]{0,1:T(8,128)(2,1)S(1)} %reshape.353), channel_id=1, source_target_pairs={{0,1},{1,0},{2,3},{3,2},{4,5},{5,4},{6,7},{7,6},{8,9},{9,8},{10,11... | collective-permute-start | bytes 1769480 | tf_op jit(solution)/shard_map/ppermute | solution.py:761
  399.2 2.7 collective-permute-start.17
  422.1 32.8 %collective-permute-start.5 = (bf16[320,768]{1,0:T(8,128)(2,1)}, bf16[320,768]{1,0:T(8,128)(2,1)}, u32[]{:S(2)}, u32[]{:S(2)}) collective-permute-start(bf16[320,768]{1,0:T(8,128)(2,1)} %slice.645), channel_id=1, source_target_pairs={{0,8},{8,0},{1,9},{9,1},{2,10},{10,2},{3,11},{11,3},{4,12},{12,4},... | collective-permute-start | bytes 1474568 | tf_op jit(solution)/shard_map/ppermute | solution.py:761
  426.3 39.0 %all-to-all-start.11 = ((bf16[4,192,1024]{2,1,0:T(8,128)(2,1)}), bf16[4,192,1024]{2,1,0:T(8,128)(2,1)S(1)}, u32[]{:S(2)}, u32[]{:S(2)}) async-start(bf16[4,192,1024]{2,1,0:T(8,128)(2,1)} %bitcast.274), calls=%async_computation.11 | async-start | bytes 3145728 | tf_op jit(solution)/shard_map/all_to_all | solution.py:959
  434.0 20.9 %copy-start.41 = (f32[640,768]{1,0:T(8,128)S(1)}, f32[640,768]{1,0:T(8,128)}, u32[]{:S(2)}) copy-start(f32[640,768]{1,0:T(8,128)} %copy-done.40) | copy-start | bytes 5898244
  434.0 38.4 %collective-permute-start.23 = (bf16[576,512]{1,0:T(8,128)(2,1)}, bf16[576,512]{1,0:T(8,128)(2,1)}, u32[]{:S(2)}, u32[]{:S(2)}) collective-permute-start(bf16[576,512]{1,0:T(8,128)(2,1)} %dynamic-slice_convert_fusion), channel_id=1, source_target_pairs={{0,2},{1,3},{2,0},{3,1},{4,6},{5,7},{6,4},{7,5},{8,10},{9,11},{10,... | collective-permute-start | bytes 1769480 | tf_op jit(solution)/shard_map/ppermute | solution.py:761
  465.3 52.4 %all-to-all-start.13 = ((bf16[4,192,1024]{2,1,0:T(8,128)(2,1)}), bf16[4,192,1024]{2,1,0:T(8,128)(2,1)}, u32[]{:S(2)}, u32[]{:S(2)}) async-start(bf16[4,192,1024]{2,1,0:T(8,128)(2,1)} %bitcast.273), calls=%async_computation.13 | async-start | bytes 3145728 | tf_op jit(solution)/shard_map/all_to_all | solution.py:959
  470.5 26.1 %collective-permute-start.6 = (bf16[160,768]{1,0:T(8,128)(2,1)}, bf16[160,768]{1,0:T(8,128)(2,1)}, u32[]{:S(2)}, u32[]{:S(2)}) collective-permute-start(bf16[160,768]{1,0:T(8,128)(2,1)} %get-tuple-element.100), channel_id=1, source_target_pairs={{0,16},{16,0},{1,17},{17,1},{2,18},{18,2},{3,19},{19,3},{4,20},{20... | collective-permute-start | bytes 737288 | tf_op jit(solution)/shard_map/ppermute | solution.py:761
  475.9 38.1 %collective-permute-start.24 = (bf16[288,512]{1,0:T(8,128)(2,1)}, bf16[288,512]{1,0:T(8,128)(2,1)}, u32[]{:S(2)}, u32[]{:S(2)}) collective-permute-start(bf16[288,512]{1,0:T(8,128)(2,1)} %dynamic-slice_convert_fusion.2), channel_id=1, source_target_pairs={{0,4},{1,5},{2,6},{3,7},{4,0},{5,1},{6,2},{7,3},{8,12},{9,13},{10,... | collective-permute-start | bytes 884744 | tf_op jit(solution)/shard_map/ppermute | solution.py:761
  478.2 25.7 %copy-start.20 = (f32[256,768]{0,1:T(8,128)}, f32[256,768]{0,1:T(8,128)S(1)}, u32[]{:S(2)}) copy-start(f32[256,768]{0,1:T(8,128)S(1)} %fusion.156) | copy-start | bytes 2359300
  479.0 64.3 %collective-permute-start.2 = (bf16[128,768]{0,1:T(8,128)(2,1)}, bf16[128,768]{0,1:T(8,128)(2,1)}, u32[]{:S(2)}, u32[]{:S(2)}) collective-permute-start(bf16[128,768]{0,1:T(8,128)(2,1)} %slice.647), channel_id=1, source_target_pairs={{0,1},{1,0},{2,3},{3,2},{4,5},{5,4},{6,7},{7,6},{8,9},{9,8},{10,11... | collective-permute-start | bytes 589832 | tf_op jit(solution)/shard_map/ppermute | solution.py:761
  515.2 22.4 %collective-permute-start.25 = (bf16[288,512]{1,0:T(8,128)(2,1)S(1)}, bf16[288,512]{1,0:T(8,128)(2,1)}, u32[]{:S(2)}, u32[]{:S(2)}) collective-permute-start(bf16[288,512]{1,0:T(8,128)(2,1)S(1)} %add_convert_fusion), channel_id=1, source_target_pairs={{0,4},{1,5},{2,6},{3,7},{4,0},{5,1},{6,2},{7,3},{8,12},{9,13},{10,... | collective-permute-start | bytes 884744 | tf_op jit(solution)/shard_map/ppermute | solution.py:761
  517.7 25.5 %all-to-all-start.6 = ((bf16[8,40,768]{2,1,0:T(8,128)(2,1)}), bf16[8,40,768]{2,1,0:T(8,128)(2,1)S(1)}, u32[]{:S(2)}, u32[]{:S(2)}) async-start(bf16[8,40,768]{2,1,0:T(8,128)(2,1)} %pad_maximum_fusion.9), calls=%async_computation.6 | async-start | bytes 983040 | tf_op jit(solution)/shard_map/all_to_all | solution.py:876
  539.5 16.6 %collective-permute-start.26 = (bf16[576,512]{1,0:T(8,128)(2,1)}, bf16[576,512]{1,0:T(8,128)(2,1)}, u32[]{:S(2)}, u32[]{:S(2)}) collective-permute-start(bf16[576,512]{1,0:T(8,128)(2,1)} %pad_maximum_fusion.7), channel_id=1, source_target_pairs={{0,2},{1,3},{2,0},{3,1},{4,6},{5,7},{6,4},{7,5},{8,10},{9,11},{10,... | collective-permute-start | bytes 1769480 | tf_op jit(solution)/shard_map/ppermute | solution.py:761
  546.6 14.4 %collective-permute-start.18 = (bf16[200,768]{1,0:T(8,128)(2,1)S(1)}, bf16[200,768]{1,0:T(8,128)(2,1)S(1)}, u32[]{:S(2)}, u32[]{:S(2)}) collective-permute-start(bf16[200,768]{1,0:T(8,128)(2,1)S(1)} %dynamic-slice_convert_fusion.1), channel_id=1, source_target_pairs={{0,2},{1,3},{2,0},{3,1},{4,6},{5,7},{6,4},{7,5},{8,10},{9,11},{10,... | collective-permute-start | bytes 921608 | tf_op jit(solution)/shard_map/ppermute | solution.py:761
  558.6 22.8 %collective-permute-start.27 = (bf16[1152,512]{1,0:T(8,128)(2,1)}, bf16[1152,512]{1,0:T(8,128)(2,1)}, u32[]{:S(2)}, u32[]{:S(2)}) collective-permute-start(bf16[1152,512]{1,0:T(8,128)(2,1)} %pad_maximum_fusion.2), channel_id=1, source_target_pairs={{0,1},{1,0},{2,3},{3,2},{4,5},{5,4},{6,7},{7,6},{8,9},{9,8},{10,11... | collective-permute-start | bytes 3538952 | tf_op jit(solution)/shard_map/ppermute | solution.py:761
  561.1 10.5 %collective-permute-start.19 = (bf16[100,768]{1,0:T(8,128)(2,1)S(1)}, bf16[100,768]{1,0:T(8,128)(2,1)S(1)}, u32[]{:S(2)}, u32[]{:S(2)}) collective-permute-start(bf16[100,768]{1,0:T(8,128)(2,1)S(1)} %dynamic-slice_convert_fusion.3), channel_id=1, source_target_pairs={{0,4},{1,5},{2,6},{3,7},{4,0},{5,1},{6,2},{7,3},{8,12},{9,13},{10,... | collective-permute-start | bytes 460808 | tf_op jit(solution)/shard_map/ppermute | solution.py:761
  571.6 9.6 %collective-permute-start.20 = (bf16[100,768]{1,0:T(8,128)(2,1)S(1)}, bf16[100,768]{1,0:T(8,128)(2,1)S(1)}, u32[]{:S(2)}, u32[]{:S(2)}) collective-permute-start(bf16[100,768]{1,0:T(8,128)(2,1)S(1)} %add_convert_fusion.1), channel_id=1, source_target_pairs={{0,4},{1,5},{2,6},{3,7},{4,0},{5,1},{6,2},{7,3},{8,12},{9,13},{10,... | collective-permute-start | bytes 460808 | tf_op jit(solution)/shard_map/ppermute | solution.py:761
  581.4 6.9 %collective-permute-start.21 = (bf16[200,768]{1,0:T(8,128)(2,1)S(1)}, bf16[200,768]{1,0:T(8,128)(2,1)S(1)}, u32[]{:S(2)}, u32[]{:S(2)}) collective-permute-start(bf16[200,768]{1,0:T(8,128)(2,1)S(1)} %pad_maximum_fusion.14), channel_id=1, source_target_pairs={{0,2},{1,3},{2,0},{3,1},{4,6},{5,7},{6,4},{7,5},{8,10},{9,11},{10,... | collective-permute-start | bytes 921608 | tf_op jit(solution)/shard_map/ppermute | solution.py:761
  588.5 3.5 collective-permute-start.22
  (74 other events, 433.9 us)
Sparse Core Ops, SparseCore 0:
  11.9 40.5 all-gather.6
  54.9 56.6 all-gather.8
  113.5 44.0 all-gather.10
  191.1 41.4 reduce-scatter.13
  301.9 45.1 reduce-scatter.11
  416.0 69.8 reduce-scatter.9
